TPU v7x, 256 devices: a whole 4x4x8 slice. The times are simulated.
256 devices in a mesh: dp: 64 (over z, x, core), seq: 4 (over y).
Axes of the slice: x: 4, y: 4, z: 8, core: 2. Of those that a mesh axis runs over, the one named last changes fastest.
Arguments:
- hidden_in: bfloat16 [65536, 4096], P(('dp', 'seq')), may hold values from -24 to 24
- bc_weight: bfloat16 [4096, 256], P('dp'), may hold values from -0.09375 to 0.09375
- values: bfloat16 [65536, 4096], P(('dp', 'seq')), may hold values from -6 to 6
- teacher: bfloat16 [65536, 4096], P(('dp', 'seq')), may hold values from -6 to 6
- decay_codes: int32 [65536, 64], P(('dp', 'seq')), may hold values from 0 to 15
- resets: int32 [65536], P(('dp', 'seq')), may hold values 0 or 1
- head_decay_rates: float32 [64], replicated, may hold values from 0.25 to 100
- skip_gain: float32 [64], replicated, may hold values from 0.5 to 1.5
- confidence: int32 [65536], P(('dp', 'seq')), may hold values from 1 to 8
Outputs:
- values_grad: bfloat16 [65536, 4096], P(('dp', 'seq'))
- hidden_grad: bfloat16 [65536, 4096], P(('dp', 'seq'))
- weight_grad: float32 [4096, 256], P('dp')
All inputs are finite; a program needn't handle non-finite values. No bound on the sum of `resets` on one device may be relied on, other than what follows from the above.
Results may differ from a plain program's by a relative error of at most 0.011.
Values may be sent and summed in bfloat16 or wider, within the bound.
No kernel may reach another device: no remote copies, remote signals or barrier semaphores. Data moves between devices by JAX's collectives and lax.ppermute only.
A program may use at most 128 MiB of HBM per device.

v0:
```python
import math

import jax
import jax.numpy as jnp
from jax import lax
from jax.sharding import PartitionSpec as P

GROUP = 256


SPIKE_MULTIPLIER = 3000.0
STEP_FACTOR = 16.0


def carried_in(x, axis, combine, identity):
    peers, place = (lax.axis_size(axis), lax.axis_index(axis))
    everything = jax.tree.map(lambda part: lax.all_gather(part, axis), x)
    start = jax.tree.map(
        lambda part, zero: jnp.broadcast_to(jnp.asarray(zero, part.dtype), part.shape), x, identity
    )

    def carried_step(k, before):
        reached = k < place
        new = combine(before, jax.tree.map(lambda part: part[k], everything))
        return jax.tree.map(lambda a, b: jnp.where(reached, a, b), new, before)

    return lax.fori_loop(0, peers, carried_step, start)


def prefix(x, axis, combine, identity):
    peers, place = (lax.axis_size(axis), lax.axis_index(axis))
    everything = jax.tree.map(
        lambda part, kind: lax.all_gather(part.astype(kind), axis), x, (jnp.bfloat16, jnp.bfloat16)
    )
    start = jax.tree.map(
        lambda part, zero: jnp.broadcast_to(jnp.asarray(zero, part.dtype), part.shape), x, identity
    )

    def prefix_step(k, before):
        at = peers - 1 - k
        reached = at > place
        new = combine(
            before, jax.tree.map(lambda part, own: part[at].astype(own.dtype), everything, x)
        )
        return jax.tree.map(lambda a, b: jnp.where(reached, a, b), new, before)

    return lax.fori_loop(0, peers, prefix_step, start)


def decay_terms(decay_codes, resets, head_decay_rates):
    logarithm_floor = jnp.log(0.9995 + 0.0004 * decay_codes.astype(jnp.float32) / 15.0)
    decay_logarithm = (
        head_decay_rates[None, :]
        * (1.0 + SPIKE_MULTIPLIER * resets.astype(jnp.float32))[:, None]
        * logarithm_floor
    )
    return (decay_logarithm, -STEP_FACTOR * logarithm_floor)


def combine(earlier, later):
    return (earlier[0] + later[0], jnp.exp(later[0])[:, None, None] * earlier[1] + later[1])


def body(
    hidden_in,
    bc_weight,
    values,
    teacher,
    decay_codes,
    resets,
    head_decay_rates,
    skip_gain,
    confidence,
):
    length = hidden_in.shape[0]
    blocks = length // GROUP
    head_count = decay_codes.shape[1]
    head_size = values.shape[1] // head_count
    state_size = bc_weight.shape[1] // 2
    seq_count = lax.axis_size("seq")
    doc_len = length * seq_count
    all_tokens = doc_len * lax.axis_size("dp")
    conf_float = confidence.astype(jnp.float32)
    conf_total = lax.psum(jnp.sum(conf_float), "seq")
    full_weight = lax.all_gather(bc_weight, "dp", axis=0, tiled=True)
    bc_acc = jnp.dot(hidden_in, full_weight, preferred_element_type=jnp.float32)
    bc_rows = bc_acc.astype(jnp.bfloat16).reshape(blocks, GROUP, 2 * state_size)
    input_map = bc_rows[:, :, :state_size]
    output_map = bc_rows[:, :, state_size:]
    decay_logarithm, step_size = decay_terms(decay_codes, resets, head_decay_rates)
    cumulative = jnp.cumsum(decay_logarithm.reshape(blocks, GROUP, head_count), axis=1)
    step_blk = step_size.reshape(blocks, GROUP, head_count)
    block_log = cumulative[:, -1, :]
    tail_decay = jnp.exp(block_log[:, None, :] - cumulative)
    leading_decay = jnp.exp(cumulative)
    cum_heads = jnp.transpose(cumulative, (0, 2, 1))
    lower_tri = lax.broadcasted_iota(jnp.int32, (GROUP, GROUP), 0) >= lax.broadcasted_iota(
        jnp.int32, (GROUP, GROUP), 1
    )
    spread = jnp.where(lower_tri, cum_heads[:, :, :, None] - cum_heads[:, :, None, :], 0.0)
    decay_grid = (
        jnp.where(lower_tri, jnp.exp(spread), 0.0)
        * jnp.transpose(step_blk, (0, 2, 1))[:, :, None, :]
    )
    intersection = jnp.einsum(
        "btn,bsn->bts", output_map, input_map, preferred_element_type=jnp.float32
    )
    mixing = (intersection[:, None] * decay_grid).astype(jnp.bfloat16)
    value_blocks = values.reshape(blocks, GROUP, head_count, head_size)
    write_scale = tail_decay * step_blk
    value_scaled = (write_scale[..., None] * value_blocks).astype(jnp.bfloat16)
    local_state = jnp.einsum(
        "bshp,bsn->bhpn", value_scaled, input_map, preferred_element_type=jnp.float32
    )
    zero_state = jnp.zeros((head_count, head_size, state_size), jnp.float32)
    zero_log = jnp.zeros((head_count,), jnp.float32)
    running_state = zero_state
    running_log = zero_log
    position = 0
    prefix_states = running_state
    prefix_logs = running_log
    running_state = (
        jnp.exp(block_log[position])[:, None, None] * running_state + local_state[position]
    )
    running_log = block_log[position]
    device_log = running_log
    entry_device = carried_in((device_log, running_state), "seq", combine, (zero_log, zero_state))[
        1
    ]
    entry_state = jnp.stack([jnp.exp(prefix_logs)[:, None, None] * entry_device + prefix_states])
    entry_bf = entry_state.astype(jnp.bfloat16)
    outputs = jnp.einsum(
        "bhts,bshp->bthp", mixing, value_blocks, preferred_element_type=jnp.float32
    )
    outputs = outputs + leading_decay[..., None] * jnp.einsum(
        "btn,bhpn->bthp", output_map, entry_bf, preferred_element_type=jnp.float32
    )
    outputs = outputs + skip_gain[None, None, :, None] * value_blocks
    token_weight = conf_float * doc_len / conf_total
    target = teacher.reshape(blocks, GROUP, head_count, head_size)
    out_grad = (token_weight.reshape(blocks, GROUP)[:, :, None, None] * (outputs - target)).astype(
        jnp.bfloat16
    )
    out_scaled = (leading_decay[..., None] * out_grad).astype(jnp.bfloat16)
    state_pull = jnp.einsum(
        "bthp,btn->bhpn", out_scaled, output_map, preferred_element_type=jnp.float32
    )
    suffix_grads = [zero_state] * blocks
    suffix_logs = [zero_log] * blocks
    running_grad = zero_state
    running_log = zero_log
    position = 0
    suffix_grads[position] = running_grad
    suffix_logs[position] = running_log
    running_grad = jnp.exp(block_log[position])[:, None, None] * running_grad + state_pull[position]
    after_grad = prefix((device_log, running_grad), "seq", combine, (zero_log, zero_state))[1]
    exit_grad = jnp.stack([jnp.exp(suffix_logs[0])[:, None, None] * after_grad + suffix_grads[0]])
    exit_bf = exit_grad.astype(jnp.bfloat16)
    pair_dots = jnp.einsum(
        "bthp,bshp->bhts", out_grad, value_blocks, preferred_element_type=jnp.float32
    )
    score_grad = jnp.sum(pair_dots * decay_grid, axis=1).astype(jnp.bfloat16)
    values_grad = jnp.einsum(
        "bhts,bthp->bshp", mixing, out_grad, preferred_element_type=jnp.float32
    )
    values_grad = values_grad + write_scale[..., None] * jnp.einsum(
        "bsn,bhpn->bshp", input_map, exit_bf, preferred_element_type=jnp.float32
    )
    values_grad = values_grad + skip_gain[None, None, :, None] * out_grad
    input_grad = jnp.einsum(
        "bts,btn->bsn", score_grad, output_map, preferred_element_type=jnp.float32
    )
    input_grad = input_grad + jnp.einsum(
        "bshp,bhpn->bsn", value_scaled, exit_bf, preferred_element_type=jnp.float32
    )
    output_grad = jnp.einsum(
        "bts,bsn->btn", score_grad, input_map, preferred_element_type=jnp.float32
    )
    output_grad = output_grad + jnp.einsum(
        "bthp,bhpn->btn", out_scaled, entry_bf, preferred_element_type=jnp.float32
    )
    bc_grad = (
        jnp.concatenate([input_grad, output_grad], axis=2)
        .reshape(length, 2 * state_size)
        .astype(jnp.bfloat16)
    )
    contract_cols = (((1,), (1,)), ((), ()))
    hidden_acc = lax.dot_general(
        bc_grad, full_weight, contract_cols, preferred_element_type=jnp.float32
    )
    hidden_grad = hidden_acc.astype(jnp.bfloat16)
    contract_rows = (((0,), (0,)), ((), ()))
    local_rows = bc_weight.shape[0]
    full_term = lax.dot_general(
        hidden_in, bc_grad, contract_rows, preferred_element_type=jnp.float32
    )
    summed = lax.psum(full_term, ("dp", "seq"))
    own_rows = lax.dynamic_slice_in_dim(summed, lax.axis_index("dp") * local_rows, local_rows, 0)
    weight_grad = own_rows / math.sqrt(all_tokens)
    return (
        values_grad.reshape(length, head_count * head_size).astype(jnp.bfloat16),
        hidden_grad,
        weight_grad,
    )


def solution(mesh):
    return jax.shard_map(
        body,
        mesh=mesh,
        in_specs=(
            P(("dp", "seq"), None),
            P("dp", None),
            P(("dp", "seq"), None),
            P(("dp", "seq"), None),
            P(("dp", "seq"), None),
            P(("dp", "seq")),
            P(),
            P(),
            P(("dp", "seq")),
        ),
        out_specs=(P(("dp", "seq"), None), P(("dp", "seq"), None), P("dp", None)),
        check_vma=False,
    )
```

profile of v0, /device:TPU:2, one launch (start us, length us, event | category | flops | bytes accessed | tf_op | source)
XLA Modules:
  0.0 555.4 jit_solution(11231758227764263669)
XLA Ops:
  7.2 0.7 all-gather.8.cloned.1.call-update
  8.0 0.9 copy.61
  8.9 0.7 multiply_add_fusion
  9.6 0.8 multiply_bitcast_fusion
  10.4 0.6 reduce-window.6
  11.6 4.1 copy.66
  15.7 3.3 fusion.11
  19.0 71.0 %all-gather.8.cloned.1.call-done = bf16[4096,256]{1,0:T(8,128)(2,1)} async-done(((bf16[64,256]{1,0:T(8,128)(2,1)}), bf16[4096,256]{1,0:T(8,128)(2,1)}) %all-gather.8.cloned.1.call-update) | async-done | bytes 2097168 | tf_op jit(solution)/shard_map/all_gather | solution.py:85
  90.1 2.4 fusion.24
  92.5 2.1 convolution_add_fusion
  94.7 0.6 copy-done.8
  95.3 0.6 convert_reduce_fusion
  95.9 11.1 %psum.14 = f32[]{:T(128)} all-reduce(f32[]{:T(128)} %convert_reduce_fusion), channel_id=1, replica_groups=mesh['dp'=64,'seq'=4] {'seq'}, use_global_device_ids=true, to_apply=%region_1.0 | all-reduce | flops 1 | bytes 8 | tf_op jit(solution)/shard_map/psum | solution.py:84
  107.3 4.4 copy.72
  111.8 6.9 %all-gather = f32[4,1,64]{2,1,0:T(1,128)S(1)} all-gather(f32[1,1,64]{2,1,0:T(1,128)S(1)} %get-tuple-element.317), channel_id=2, replica_groups=mesh['dp'=64,'seq'=4] {'seq'}, dimensions={0}, use_global_device_ids=true | all-gather | bytes 1280 | tf_op jit(solution)/shard_map/all_gather | solution.py:17
  118.7 0.7 multiply_divide_fusion
  119.6 59.5 %all-gather.10.cloned.1.call-done = f32[256,64,128]{2,1,0:T(8,128)} async-done(((f32[64,64,128]{2,1,0:T(8,128)}), f32[256,64,128]{2,1,0:T(8,128)}) %all-gather.10.cloned.1.call-update) | async-done | bytes 8388624 | tf_op jit(solution)/shard_map/all_gather | solution.py:17
  179.1 14.9 %while.30 = (s32[]{:T(128)}, f32[64,64,128]{2,1,0:T(8,128)}, s32[]{:T(128)}, f32[4,64]{1,0:T(4,128)S(1)}, f32[4,64,64,128]{3,2,1,0:T(8,128)}, /*index=5*/s32[]{:T(128)}, s32[]{:T(128)}) while((s32[]{:T(128)}, f32[64,64,128]{2,1,0:T(8,128)}, s32[]{:T(128)}, f32[4,64]{1,0:T(4,128)S(1)}, f32[4,64,64,128]{3,2,1,0:T(8,128)}, ...), condition=%wide.region_5.6_spmd.clone, body=%wide.region_4.5_spmd.clone.sunk | while | flops 2097156 | bytes 6292329 | solution.py:27
  179.1 3.2 fusion.71
  182.4 3.9 fusion.71
  186.3 3.9 fusion.71
  190.2 3.9 fusion.71
  194.0 2.4 fusion.33
  196.5 1.0 copy-done.4
  197.5 6.2 %fusion.10 = bf16[1,256,64,64]{1,3,2,0:T(8,128)(2,1)S(1)} fusion(f32[1,256,64,64]{1,3,2,0:T(8,128)S(1)} %bitcast.161, f32[256,64,64]{0,2,1:T(8,128)S(1)} %fusion.33, bf16[256,64,64]{0,2,1:T(8,128)(2,1)S(1)} %bitcast.157, f32[64,256]{1,0:T(8,128)S(1)} %copy.65, f32[64,256]{1,0:T(8,128)S(1)} %bitcast_add_fusion.4, f32[256,256]{1,0:T(8,128)S(1)} %fusion.41, ...), kind=kOutput, calls=%fused_computation.23 | convolution fusion | flops 570425344 | bytes 15205632 | tf_op jit(solution)/shard_map/bhts,bshp->bthp/dot_general | solution.py:132
  203.7 1.3 copy-done.5
  205.0 1.7 add_convert_fusion
  206.8 8.8 %all-gather.3 = bf16[4,1,64]{2,1,0:T(2,128)(2,1)S(1)} all-gather(bf16[1,1,64]{2,1,0:T(2,128)(2,1)S(1)} %slice.61), channel_id=5, replica_groups=mesh['dp'=64,'seq'=4] {'seq'}, dimensions={0}, use_global_device_ids=true | all-gather | bytes 640 | tf_op jit(solution)/shard_map/all_gather | solution.py:33
  215.6 3.0 fusion.21
  218.6 0.5 copy-done.6
  219.1 6.9 %multiply_reduce_fusion = bf16[256,256]{1,0:T(8,128)(2,1)S(1)} fusion(bf16[256,64,64]{0,2,1:T(8,128)(2,1)S(1)} %bitcast.159, f32[64,256]{1,0:T(8,128)S(1)} %copy.65, f32[64,256]{1,0:T(8,128)S(1)} %bitcast_add_fusion.4, pred[256,256]{1,0:T(8,128)(4,1)S(1)} %iota_compare_fusion, bf16[1,256,64,64]{1,3,2,0:T(8,128)(2,1)S(1)} %copy-done.6), kind=kOutput, calls=%fused_computation.6 | convolution fusion | flops 561971200 | bytes 4521984 | tf_op jit(solution)/shard_map/bthp,bshp->bhts/dot_general | solution.py:159
  226.0 0.2 fusion.27
  226.3 32.4 %all-gather.12.cloned.1.call-done = bf16[256,64,128]{2,1,0:T(8,128)(2,1)} async-done(((bf16[64,64,128]{2,1,0:T(8,128)(2,1)}), bf16[256,64,128]{2,1,0:T(8,128)(2,1)}) %all-gather.12.cloned.1.call-update) | async-done | bytes 4194320 | tf_op jit(solution)/shard_map/all_gather | solution.py:33
  258.7 13.7 %while.31 = (s32[]{:T(128)}, f32[64,64,128]{2,1,0:T(8,128)}, s32[]{:T(128)}, bf16[4,64]{1,0:T(4,128)(2,1)S(1)}, bf16[4,64,64,128]{3,2,1,0:T(8,128)(2,1)}, /*index=5*/s32[]{:T(128)}, s32[]{:T(128)}, s32[]{:T(128)}, s32[]{:T(128)}) while((s32[]{:T(128)}, f32[64,64,128]{2,1,0:T(8,128)}, s32[]{:T(128)}, bf16[4,64]{1,0:T(4,128)(2,1)S(1)}, ...), condition=%wide.region_7.8_spmd.clone, body=%wide.region_6.7_spmd.clone.sunk | while | flops 2621512 | bytes 5243687 | solution.py:47
  258.7 3.0 fusion.72
  261.7 3.6 fusion.72
  265.2 3.6 fusion.72
  268.8 3.6 fusion.72
  272.4 2.8 convolution_bitcast_fusion.1
  275.2 0.2 fusion.28
  275.4 2.7 convolution_bitcast_fusion
  278.1 2.4 fusion.30
  280.6 6.8 %fusion.6 = bf16[1,256,64,64]{1,3,2,0:T(8,128)(2,1)} fusion(bf16[1,256,64,64]{1,3,2,0:T(8,128)(2,1)S(1)} %copy-done.7, f32[256,64,64]{0,2,1:T(8,128)S(1)} %fusion.30, f32[64,256]{1,0:T(8,128)S(1)} %copy.65, f32[64,256]{1,0:T(8,128)S(1)} %bitcast_add_fusion.4, f32[256,256]{1,0:T(8,128)S(1)} %fusion.41, pred[256,256]{1,0:T(8,128)(4,1)S(1)} %iota_compare_fusion, ...), kind=kOutput, calls=%fused_computation.17 | convolution fusion | flops 568328192 | bytes 8913152 | tf_op jit(solution)/shard_map/bhts,bthp->bshp/dot_general | solution.py:163
  287.4 4.1 copy.74
  291.5 3.7 convolution_convert_fusion
  295.2 252.0 %all-reduce.2.cloned.1.call-done = f32[4096,256]{0,1:T(8,128)} async-done(((f32[4096,256]{0,1:T(8,128)}), f32[4096,256]{0,1:T(8,128)}) %all-reduce.2.cloned.1.call-update) | async-done | bytes 4194320 | tf_op jit(solution)/shard_map/psum | solution.py:197
  547.2 1.0 dynamic-slice_multiply_fusion
  548.2 0.7 copy.75
  (54 shorter events, 1.4 us)
Async XLA Ops:
  7.2 82.9 %copy-start = (bf16[256,4096]{1,0:T(8,128)(2,1)S(1)}, bf16[256,4096]{1,0:T(8,128)(2,1)}, u32[]{:S(2)}) copy-start(bf16[256,4096]{1,0:T(8,128)(2,1)} %param.13) | copy-start | bytes 6291460
  7.2 82.9 %all-gather.8.cloned.1.call-start = ((), (), s32[]{:S(2)}) async-start(), calls=%async_computation | async-start | bytes 2129920 | tf_op jit(solution)/shard_map/all_gather | solution.py:85
  7.9 171.2 %all-gather.10.cloned.1.call-start = ((), (), s32[]{:S(2)}) async-start(), calls=%async_computation.2 | async-start | bytes 10485760 | tf_op jit(solution)/shard_map/all_gather | solution.py:17
  90.1 2.5 copy-start.1
  94.6 0.7 copy-start.8
  94.6 164.1 %all-gather.12.cloned.1.call-start = ((), (), s32[]{:S(2)}) async-start(), calls=%async_computation.3 | async-start | bytes 5242880 | tf_op jit(solution)/shard_map/all_gather | solution.py:33
  194.0 2.5 copy-start.2
  194.0 3.5 copy-start.4
  194.0 3.5 copy-start.9
  203.7 1.4 copy-start.5
  206.7 340.5 %all-reduce.2.cloned.1.call-start = ((), (), s32[]{:S(2)}) async-start(), calls=%async_computation.1 | async-start | bytes 8388608 | tf_op jit(solution)/shard_map/psum | solution.py:197
  215.6 3.0 copy-start.3
  215.6 3.5 copy-start.6
  278.1 2.5 copy-start.7
Sparse Core Ops, SparseCore 0:
  10.8 79.2 all-gather.7
  94.7 84.3 all-gather.9
  206.9 51.7 all-gather.11
  278.2 268.8 all-reduce.1
where the time goes:
time: 556 us; the launch traced here: 555 us
  waiting for transfers between devices  416 us (75%)
  matrix products  43.8 us (8%)
  other arithmetic  36.4 us (7%)
  blocking collectives  26.8 us (5%)
  local copies, waits for them, and re-layouts  18.5 us (3%)
  between operations  14 us (3%)
    psum x1, waiting for transfers between devices, body(): summed = lax.psum(full_term, ('dp', 'seq'))  252 us
    all_gather x1, waiting for transfers between devices, body(): full_weight = lax.all_gather(bc_weight, 'dp', axis=0, tiled=True)  71 us
    all_gather x1, waiting for transfers between devices, carried_in(): everything = jax.tree.map(lambda part: lax.all_gather(part, axis), x)  59.5 us
    all_gather x1, waiting for transfers between devices, prefix(): lax.all_gather(part.astype(kind), axis)  32.4 us
    select_n x4, other arithmetic, carried_step(): return jax.tree.map(lambda a, b: jnp.where(reached, a, b), new, before)  14.9 us
    select_n x4, other arithmetic, prefix_step(): return jax.tree.map(lambda a, b: jnp.where(reached, a, b), new, before)  13.7 us
    unnamed x25, local copies, waits for them, and re-layouts  13.3 us
    psum x1, blocking collectives, body(): conf_total = lax.psum(jnp.sum(conf_float), 'seq')  11.1 us
  transfers between devices with their start and end apart: 4, of which 4 were waited for; matrix products, arithmetic and copies ran while one was open for 8% of the time, Pallas kernels for 0%

commit v1 on v0

v1 whole, which is shorter than its diff:
```python
import functools
import math

import jax
import jax.numpy as jnp
from jax import lax
from jax.experimental import pallas as pl
from jax.experimental.pallas import tpu as pltpu
from jax.sharding import PartitionSpec as P

BF = jnp.bfloat16
F32 = jnp.float32
BLOCK = 256
HEAD = 64
STATE = 128
PEERS = 4
LOCAL_HEADS = 16
WIDE = LOCAL_HEADS * HEAD
SPIKE_MULTIPLIER = 3000.0
STEP_FACTOR = 16.0
ZREL = (0, 4, 2, 6, 1, 5, 3, 7)
MIB = 1 << 20


def over_dp(x, mask):
    return lax.ppermute(x, "dp", [(i, i ^ mask) for i in range(64)])


def over_seq(x, mask):
    return lax.ppermute(x, "seq", [(i, i ^ mask) for i in range(4)])


def dot_nn(a, b):
    return lax.dot_general(a, b, (((1,), (0,)), ((), ())), preferred_element_type=F32)


def dot_nt(a, b):
    return lax.dot_general(a, b, (((1,), (1,)), ((), ())), preferred_element_type=F32)


def dot_tn(a, b):
    return lax.dot_general(a, b, (((0,), (0,)), ((), ())), preferred_element_type=F32)


def vmem():
    return pl.BlockSpec(memory_space=pltpu.VMEM)


def anywhere():
    return pl.BlockSpec(memory_space=pl.ANY)


def smem():
    return pl.BlockSpec(memory_space=pltpu.SMEM)


def decay_kernel(small_ref, grid_ref, lead_ref, write_ref):
    small = small_ref[0]
    cum_rows = small[0:LOCAL_HEADS]
    step_rows = small[LOCAL_HEADS : 2 * LOCAL_HEADS]
    lead_rows = jnp.exp(cum_rows)
    write_rows = jnp.exp(cum_rows[:, BLOCK - 1 : BLOCK] - cum_rows) * step_rows
    columns = jnp.concatenate([cum_rows, lead_rows, write_rows], axis=0).T
    lower = lax.broadcasted_iota(jnp.int32, (BLOCK, BLOCK), 0) >= lax.broadcasted_iota(
        jnp.int32, (BLOCK, BLOCK), 1
    )
    first = lax.broadcasted_iota(jnp.int32, (BLOCK, 2 * HEAD), 1) < HEAD
    for h in range(LOCAL_HEADS):
        spread = jnp.where(lower, columns[:, h : h + 1] - cum_rows[h : h + 1, :], -1e30)
        grid_ref[0, h] = (jnp.exp(spread) * step_rows[h : h + 1, :]).astype(BF)
    for p in range(LOCAL_HEADS // 2):
        at = slice(2 * HEAD * p, 2 * HEAD * (p + 1))
        for ref, base in ((lead_ref, LOCAL_HEADS), (write_ref, 2 * LOCAL_HEADS)):
            c = base + 2 * p
            ref[0, :, at] = jnp.where(first, columns[:, c : c + 1], columns[:, c + 1 : c + 2])


def decays(small):
    blk = lambda *s: pl.BlockSpec((1, *s), lambda k: (k, *([0] * len(s))))
    return pl.pallas_call(
        decay_kernel,
        grid=(PEERS,),
        in_specs=[blk(*small.shape[1:])],
        out_specs=[blk(LOCAL_HEADS, BLOCK, BLOCK), blk(BLOCK, WIDE), blk(BLOCK, WIDE)],
        out_shape=[
            jax.ShapeDtypeStruct((PEERS, LOCAL_HEADS, BLOCK, BLOCK), BF),
            jax.ShapeDtypeStruct((PEERS, BLOCK, WIDE), F32),
            jax.ShapeDtypeStruct((PEERS, BLOCK, WIDE), F32),
        ],
        compiler_params=pltpu.CompilerParams(vmem_limit_bytes=40 * MIB),
        cost_estimate=pl.CostEstimate(flops=40_000_000, bytes_accessed=17_000_000, transcendentals=4_300_000),
        name="decays",
    )(small)


def turn_kernel(order_ref, core_ref, hidden_ref, out_ref):
    core = core_ref[0]
    turned = hidden_ref[...].T
    out_ref[core, 0] = turned[:HEAD]
    out_ref[1 - core, 0] = turned[HEAD:]


def turn(hidden, order, core):
    return pl.pallas_call(
        turn_kernel,
        grid_spec=pltpu.PrefetchScalarGridSpec(
            num_scalar_prefetch=2,
            grid=(32,),
            in_specs=[pl.BlockSpec((BLOCK, 128), lambda j, order, core: (0, order[j]))],
            out_specs=pl.BlockSpec((2, 1, 64, BLOCK), lambda j, order, core: (0, j, 0, 0)),
        ),
        out_shape=jax.ShapeDtypeStruct((2, 32, 64, BLOCK), BF),
        cost_estimate=pl.CostEstimate(flops=1000, bytes_accessed=4_200_000, transcendentals=0),
        name="turn",
    )(order, core, hidden)


def project_kernel(order_ref, core_ref, hidden_ref, *refs):
    own, other = refs[0:4], refs[4:8]
    weight_ref, rows_ref, sems = refs[8:]
    core = core_ref[0]
    copies = []
    for a in range(4):
        for side, (pieces, place) in enumerate(((own, core), (other, 1 - core))):
            for b in range(8):
                row = pl.multiple_of(order_ref[a * 8 + b] * 128 + place * 64, 64)
                copies.append(
                    pltpu.make_async_copy(
                        pieces[a].at[b], weight_ref.at[pl.ds(row, 64)], sems.at[side, a * 8 + b]
                    )
                )
                copies[-1].start()
    for c in copies:
        c.wait()
    rows_ref[...] = dot_nn(hidden_ref[...], weight_ref[...]).astype(BF)


def project(hidden, own, other, order, core):
    return pl.pallas_call(
        project_kernel,
        in_specs=[smem(), smem(), vmem()] + [anywhere()] * 8,
        out_specs=[vmem(), vmem()],
        out_shape=[
            jax.ShapeDtypeStruct((4096, 256), BF),
            jax.ShapeDtypeStruct((BLOCK, 256), BF),
        ],
        scratch_shapes=[pltpu.SemaphoreType.DMA((2, 32))],
        compiler_params=pltpu.CompilerParams(vmem_limit_bytes=32 * MIB),
        cost_estimate=pl.CostEstimate(flops=540_000_000, bytes_accessed=6_000_000, transcendentals=0),
        name="project",
    )(order, core, hidden, *own, *other)


def layer_kernel(place_ref, *refs):
    xs_in, ts_in, bcs_in = refs[0:4], refs[4:8], refs[8:12]
    grid_in, lead_in, write_in, weight_ref, keep_ref, skip_ref = refs[12:18]
    vg_out, bg_out = refs[18:22], refs[22:26]
    (x, t, bc, grid, lead, write, entry, pull, scaled, outs, acc, state, base, cross, score, ig, sem_a, sem_g) = refs[26:]
    place = place_ref[0]
    first = []
    later = []
    for k in range(PEERS):
        first.append(pltpu.make_async_copy(bcs_in[k], bc.at[k], sem_a.at[0, k]))
        first.append(pltpu.make_async_copy(xs_in[k], x.at[k], sem_a.at[1, k]))
        first.append(pltpu.make_async_copy(write_in.at[k], write.at[k], sem_a.at[2, k]))
    for k in range(PEERS):
        later.append(pltpu.make_async_copy(ts_in[k], t.at[k], sem_a.at[3, k]))
        later.append(pltpu.make_async_copy(lead_in.at[k], lead.at[k], sem_a.at[4, k]))
        later.append(pltpu.make_async_copy(grid_in.at[k], grid.at[k], sem_g.at[k]))
    for c in first + later:
        c.start()
    for c in first:
        c.wait()

    state[...] = jnp.zeros_like(state)
    for j in range(PEERS):
        k = place ^ j
        entry[k] = state[...].astype(BF)
        scaled[k] = (write[k] * x[k].astype(F32)).astype(BF)
        if j < PEERS - 1:
            state[...] = keep_ref[k] * state[...] + dot_tn(bc[k, :, :STATE], scaled[k])
    for c in later:
        c.wait()

    low = lax.broadcasted_iota(jnp.int32, (BLOCK, 2 * HEAD), 1) < HEAD

    def block(k, carry):
        b_map = bc[k, :, :STATE]
        c_map = bc[k, :, STATE:]
        cross[...] = dot_nt(c_map, b_map)
        base[...] = (
            dot_nn(c_map, entry[k]) * lead[k] + skip_ref[...] * x[k].astype(F32) - t[k].astype(F32)
        )
        score[...] = jnp.zeros_like(score)
        weight = weight_ref[k]
        for p in range(LOCAL_HEADS // 2):
            at = slice(2 * HEAD * p, 2 * HEAD * (p + 1))
            xp = x[k, :, at]
            d0 = grid[k, 2 * p].astype(F32)
            d1 = grid[k, 2 * p + 1].astype(F32)
            m0 = (cross[...] * d0).astype(BF)
            m1 = (cross[...] * d1).astype(BF)
            y = jnp.where(low, dot_nn(m0, xp), dot_nn(m1, xp))
            og = (weight * (base[:, at] + y)).astype(BF)
            zero = jnp.zeros_like(og)
            g0 = dot_nt(jnp.where(low, og, zero), xp)
            g1 = dot_nt(jnp.where(low, zero, og), xp)
            score[...] += g0 * d0 + g1 * d1
            dx = jnp.where(low, dot_tn(m0, og), dot_tn(m1, og))
            ogf = og.astype(F32)
            acc[k, :, at] = dx + skip_ref[:, at] * ogf
            outs[:, at] = (lead[k, :, at] * ogf).astype(BF)
        sg = score[...].astype(BF)
        pull[k] = dot_tn(c_map, outs[...])
        ig[k, :, STATE:] = dot_nt(outs[...], entry[k]) + dot_nn(sg, b_map)
        ig[k, :, :STATE] = dot_tn(sg, c_map)
        return carry

    lax.fori_loop(0, PEERS, block, 0)

    state[...] = jnp.zeros_like(state)
    for j in reversed(range(PEERS)):
        k = place ^ j
        leave = state[...].astype(BF)
        acc[k] = acc[k] + write[k] * dot_nn(bc[k, :, :STATE], leave)
        ig[k, :, :STATE] += dot_nt(scaled[k], leave)
        if j > 0:
            state[...] = keep_ref[k] * state[...] + pull[k]
    for k in range(PEERS):
        vg_out[k][...] = acc[k].astype(BF)
        bg_out[k][...] = ig[k].astype(bg_out[k].dtype)


def layer(place, xs, ts, bcs, grid, lead, write, weight, keep, skip):
    return pl.pallas_call(
        layer_kernel,
        in_specs=[smem()] + [anywhere()] * 15 + [vmem()] * 3,
        out_specs=[vmem()] * 8,
        out_shape=[jax.ShapeDtypeStruct((BLOCK, WIDE), BF)] * 4
        + [jax.ShapeDtypeStruct((BLOCK, 2 * STATE), F32)]
        + [jax.ShapeDtypeStruct((BLOCK, 2 * STATE), BF)] * 3,
        scratch_shapes=[
            pltpu.VMEM((PEERS, BLOCK, WIDE), BF),
            pltpu.VMEM((PEERS, BLOCK, WIDE), BF),
            pltpu.VMEM((PEERS, BLOCK, 2 * STATE), BF),
            pltpu.VMEM((PEERS, LOCAL_HEADS, BLOCK, BLOCK), BF),
            pltpu.VMEM((PEERS, BLOCK, WIDE), F32),
            pltpu.VMEM((PEERS, BLOCK, WIDE), F32),
            pltpu.VMEM((PEERS, STATE, WIDE), BF),
            pltpu.VMEM((PEERS, STATE, WIDE), F32),
            pltpu.VMEM((PEERS, BLOCK, WIDE), BF),
            pltpu.VMEM((BLOCK, WIDE), BF),
            pltpu.VMEM((PEERS, BLOCK, WIDE), F32),
            pltpu.VMEM((STATE, WIDE), F32),
            pltpu.VMEM((BLOCK, WIDE), F32),
            pltpu.VMEM((BLOCK, BLOCK), F32),
            pltpu.VMEM((BLOCK, BLOCK), F32),
            pltpu.VMEM((PEERS, BLOCK, 2 * STATE), F32),
            pltpu.SemaphoreType.DMA((5, PEERS)),
            pltpu.SemaphoreType.DMA((PEERS,)),
        ],
        compiler_params=pltpu.CompilerParams(vmem_limit_bytes=56 * MIB),
        cost_estimate=pl.CostEstimate(flops=5_000_000_000, bytes_accessed=24_000_000, transcendentals=0),
        name="layer",
    )(place, *xs, *ts, *bcs, grid, lead, write, weight, keep, skip)


def gather_heads_kernel(place_ref, p0, p1, p2, p3, out_ref, sems):
    copies = []
    for k, piece in enumerate((p0, p1, p2, p3)):
        at = pl.multiple_of((place_ref[0] ^ k) * WIDE, WIDE)
        copies.append(pltpu.make_async_copy(piece, out_ref.at[:, pl.ds(at, WIDE)], sems.at[k]))
        copies[-1].start()
    for c in copies:
        c.wait()


def gather_heads(place, pieces):
    return pl.pallas_call(
        gather_heads_kernel,
        in_specs=[smem()] + [anywhere()] * 4,
        out_specs=anywhere(),
        out_shape=jax.ShapeDtypeStruct((BLOCK, 4 * WIDE), BF),
        scratch_shapes=[pltpu.SemaphoreType.DMA((4,))],
        name="gather_heads",
    )(place, *pieces)


def body(
    hidden_in,
    bc_weight,
    values,
    teacher,
    decay_codes,
    resets,
    head_decay_rates,
    skip_gain,
    confidence,
):
    me = lax.axis_index("seq")
    dp = lax.axis_index("dp")
    place = me.astype(jnp.int32).reshape(1)
    core = (dp % 2).astype(jnp.int32).reshape(1)
    chip = dp // 2
    distance = jnp.array([z * 4 + a for a in range(4) for z in ZREL], jnp.int32)
    order = (chip ^ distance).astype(jnp.int32)
    doc_len = BLOCK * PEERS
    all_tokens = doc_len * 64

    r = bc_weight[None]
    for mask in (32, 16, 8):
        r = jnp.concatenate([r, over_dp(r, mask)], axis=0)
    own = [r] + [over_dp(r, 2 * a) for a in (1, 2, 3)]
    other = [over_dp(p, 1) for p in own]

    def exchange(array):
        cut = [
            lax.dynamic_slice_in_dim(array, (me ^ k) * WIDE, WIDE, axis=1) for k in range(PEERS)
        ]
        return [cut[0]] + [over_seq(cut[k], k) for k in (1, 2, 3)]

    conf_float = confidence.astype(F32)
    base = jnp.log(0.9995 + 0.0004 * decay_codes.astype(F32) / 15.0)
    log_decay = (
        head_decay_rates[None, :] * (1.0 + SPIKE_MULTIPLIER * resets.astype(F32))[:, None] * base
    )
    lower = (
        lax.broadcasted_iota(jnp.int32, (BLOCK, BLOCK), 0)
        >= lax.broadcasted_iota(jnp.int32, (BLOCK, BLOCK), 1)
    ).astype(F32)
    cum_rows = lax.dot_general(
        log_decay, lower, (((0,), (1,)), ((), ())), precision=lax.Precision.HIGHEST
    )
    step_rows = (-STEP_FACTOR * base).T
    packed = jnp.concatenate(
        [
            cum_rows.reshape(PEERS, LOCAL_HEADS, BLOCK),
            step_rows.reshape(PEERS, LOCAL_HEADS, BLOCK),
            jnp.broadcast_to(conf_float[None, None, :], (PEERS, 8, BLOCK)),
        ],
        axis=1,
    )
    cut = [lax.dynamic_index_in_dim(packed, me ^ k, 0, keepdims=False) for k in range(PEERS)]
    small = jnp.stack([cut[0]] + [over_seq(cut[k], k) for k in (1, 2, 3)])
    grid, lead, write = decays(small)
    conf_all = small[:, 2 * LOCAL_HEADS]
    weight = (conf_all * doc_len / jnp.sum(conf_all))[:, :, None]
    keep = jnp.repeat(jnp.exp(small[:, :LOCAL_HEADS, BLOCK - 1]), HEAD, axis=1)[:, None, :]
    skip = jnp.repeat(
        lax.dynamic_slice_in_dim(skip_gain, me * LOCAL_HEADS, LOCAL_HEADS), HEAD
    )[None, :]

    xs = exchange(values)
    ts = exchange(teacher)
    turned = turn(hidden_in, order, core)
    full_weight, rows = project(hidden_in, own, other, order, core)
    bcs = [rows] + [over_seq(rows, k) for k in (1, 2, 3)]

    outs = layer(place, xs, ts, bcs, grid, lead, write, weight, keep, skip)
    vgs, bgs = outs[:4], outs[4:]
    bc_grad = bgs[0]
    for k in (1, 2, 3):
        bc_grad = bc_grad + over_seq(bgs[k], k).astype(F32)
    bc_grad = bc_grad.astype(BF)
    pieces = [vgs[0]] + [over_seq(vgs[k], k) for k in (1, 2, 3)]

    send = dot_nn(turned[1].reshape(2048, BLOCK), bc_grad).astype(BF)
    total = dot_nn(turned[0].reshape(2048, BLOCK), bc_grad)
    total = (total + over_dp(send, 1).astype(F32)).reshape(4, 8, 64, 256)
    came = [over_dp(total[a].astype(BF), 2 * a) for a in (1, 2, 3)]
    total = total[0]
    for c in came:
        total = total + c.astype(F32)
    for mask in (8, 16, 32):
        half = total.shape[0] // 2
        total = total[:half] + over_dp(total[half:].astype(BF), mask).astype(F32)
    total = total[0]
    for mask in (1, 2):
        total = total + over_seq(total, mask)

    hidden_grad = dot_nt(bc_grad, full_weight).astype(BF)
    values_grad = gather_heads(place, pieces)
    return values_grad, hidden_grad, total / math.sqrt(all_tokens)


def solution(mesh):
    return jax.shard_map(
        body,
        mesh=mesh,
        in_specs=(
            P(("dp", "seq"), None),
            P("dp", None),
            P(("dp", "seq"), None),
            P(("dp", "seq"), None),
            P(("dp", "seq"), None),
            P(("dp", "seq")),
            P(),
            P(),
            P(("dp", "seq")),
        ),
        out_specs=(P(("dp", "seq"), None), P(("dp", "seq"), None), P("dp", None)),
        check_vma=False,
    )
```

time: 556 us -> 276 us (0.50)
  waiting for transfers between devices: 416 us -> 68.9 us
  Pallas kernels: 0 us -> 121 us
  starting transfers between devices: 0.16 us -> 51.2 us
  matrix products: 43.8 us -> 3.21 us
  other arithmetic: 36.4 us -> 3.51 us
  blocking collectives: 26.8 us -> 0 us
  between operations: 14 us -> 1.08 us
    psum x1 -> x0, waiting for transfers between devices: 252 us -> none  [body(): summed = lax.psum(full_term, ('dp', 'seq'))]
    all_gather x3 -> x0, waiting for transfers between devices: 163 us -> none  [the longest x1 71 us: body(): full_weight = lax.all_gather(bc_weight, 'dp', axis=0, tiled=True)]
    pallas_call x0 -> x5, Pallas kernels: none -> 121 us  [the longest x1 64.7 us: gather_heads(): pl.pallas_call(gather_heads_kernel, in_specs=[smem()] + [anywhere()] * 4,...]
    ppermute x0 -> x37, waiting for transfers between devices: none -> 68.9 us  [the longest x20 35 us: over_seq(): return lax.ppermute(x, 'seq', [(i, i ^ mask) for i in range(4)])]
    ppermute x0 -> x37, starting transfers between devices: none -> 51.2 us  [the longest x20 27.2 us: over_seq(): return lax.ppermute(x, 'seq', [(i, i ^ mask) for i in range(4)])]
    dot_general x15 -> x4, matrix products: 43.8 us -> 3.21 us  [the longest x1 2.07 us: dot_nt(): lax.dot_general(a, b, (((1,), (1,)), ((), ())), preferred_element_type=F32)]
    select_n x8 -> x0, other arithmetic: 28.6 us -> none  [the longest x4 14.9 us: carried_step(): return jax.tree.map(lambda a, b: jnp.where(reached, a, b), new, before)]
    all_gather x2 -> x0, blocking collectives: 15.7 us -> none  [the longest x1 8.8 us: prefix(): lax.all_gather(part.astype(kind), axis)]
  transfers between devices with their start and end apart: 4 -> 37, of which waited for: 4 -> 15; matrix products, arithmetic and copies ran while one was open for 8% -> 5% of each run, Pallas kernels for 0% -> 35%
where the time goes in v1:
time: 276 us; the launch traced here: 271 us
  Pallas kernels  121 us (44%)
  waiting for transfers between devices  68.9 us (25%)
  starting transfers between devices  51.2 us (19%)
  local copies, waits for them, and re-layouts  22.7 us (8%)
  other arithmetic  3.51 us (1%)
  matrix products  3.21 us (1%)
    pallas_call x1, Pallas kernels, gather_heads(): pl.pallas_call(gather_heads_kernel, in_specs=[smem()] + [anywhere()] * 4,...  64.7 us
    ppermute x20, waiting for transfers between devices, over_seq(): return lax.ppermute(x, 'seq', [(i, i ^ mask) for i in range(4)])  35 us
    ppermute x17, waiting for transfers between devices, over_dp(): return lax.ppermute(x, 'dp', [(i, i ^ mask) for i in range(64)])  33.8 us
    ppermute x20, starting transfers between devices, over_seq(): return lax.ppermute(x, 'seq', [(i, i ^ mask) for i in range(4)])  27.2 us
    pallas_call x1, Pallas kernels, layer(): pl.pallas_call(layer_kernel, in_specs=[smem()] + [anywhere()] * 15 + [vme...  24.8 us
    ppermute x17, starting transfers between devices, over_dp(): return lax.ppermute(x, 'dp', [(i, i ^ mask) for i in range(64)])  24 us
    pallas_call x1, Pallas kernels, turn(): pl.pallas_call(turn_kernel, grid_spec=pltpu.PrefetchScalarGridSpec(num_sc...  18.2 us
    unnamed x78, local copies, waits for them, and re-layouts  13.3 us
  transfers between devices with their start and end apart: 37, of which 15 were waited for; matrix products, arithmetic and copies ran while one was open for 5% of the time, Pallas kernels for 35%

profile of v1, /device:TPU:2, one launch (start us, length us, event | category | flops | bytes accessed | tf_op | source)
XLA Modules:
  0.0 271.3 jit_solution(4786485557306537235)
XLA Ops:
  0.6 7.3 %collective-permute-start.6 = (bf16[1,64,256]{2,1,0:T(8,128)(2,1)}, bf16[1,64,256]{2,1,0:T(8,128)(2,1)S(1)}, u32[]{:S(2)}, u32[]{:S(2)}) collective-permute-start(bf16[1,64,256]{2,1,0:T(8,128)(2,1)} %bitcast.33), channel_id=1, source_target_pairs={{0,128},{4,132},{8,136},{12,140},{16,144},{20,148},{24,152},{28,15... | collective-permute-start | bytes 98312 | tf_op jit(solution)/shard_map/ppermute | solution.py:26
  7.9 2.9 %constant_dynamic-slice_fusion.1 = (bf16[256,1024]{1,0:T(8,128)(2,1)}, bf16[256,1024]{1,0:T(8,128)(2,1)S(1)}, bf16[256,1024]{1,0:T(8,128)(2,1)}, bf16[256,1024]{1,0:T(8,128)(2,1)}) fusion(bf16[256,4096]{1,0:T(8,128)(2,1)} %param.13, s32[]{:T(128)S(6)} %select_n.46, s32[]{:T(128)S(6)} %select_n.44, s32[]{:T(128)S(6)} %select_n.43, s32[]{:T(128)S(6)} %select_n.45), kind=kLoop, calls=%fused_computation.35 | loop fusion | bytes 4194320 | tf_op jit(solution)/shard_map/dynamic_slice | solution.py:318
  10.8 1.6 collective-permute-start.3
  12.4 1.6 collective-permute-start.7
  14.3 4.1 %collective-permute-done.7 = bf16[2,64,256]{2,1,0:T(8,128)(2,1)S(1)} collective-permute-done((bf16[2,64,256]{2,1,0:T(8,128)(2,1)S(1)}, bf16[2,64,256]{2,1,0:T(8,128)(2,1)S(1)}, u32[]{:S(2)}, u32[]{:S(2)}) %collective-permute-start.7) | collective-permute-done | bytes 65568 | tf_op jit(solution)/shard_map/ppermute | solution.py:26
  18.9 4.5 %collective-permute-done.8 = bf16[4,64,256]{2,1,0:T(8,128)(2,1)S(1)} collective-permute-done((bf16[4,64,256]{2,1,0:T(8,128)(2,1)S(1)}, bf16[4,64,256]{2,1,0:T(8,128)(2,1)S(1)}, u32[]{:S(2)}, u32[]{:S(2)}) %collective-permute-start.8) | collective-permute-done | bytes 131104 | tf_op jit(solution)/shard_map/ppermute | solution.py:26
  24.1 2.4 collective-permute-start.10
  27.7 2.2 collective-permute-start.21
  29.9 3.0 %collective-permute-done.21 = f32[40,256]{1,0:T(8,128)S(1)} collective-permute-done((f32[40,256]{1,0:T(8,128)S(1)}, f32[40,256]{1,0:T(8,128)S(1)}, u32[]{:S(2)}, u32[]{:S(2)}) %collective-permute-start.21) | collective-permute-done | bytes 40992 | tf_op jit(solution)/shard_map/ppermute | solution.py:30
  32.9 4.0 %collective-permute-done.19 = f32[40,256]{1,0:T(8,128)S(1)} collective-permute-done((f32[40,256]{1,0:T(8,128)S(1)}, f32[40,256]{1,0:T(8,128)S(1)}, u32[]{:S(2)}, u32[]{:S(2)}) %collective-permute-start.19) | collective-permute-done | bytes 40992 | tf_op jit(solution)/shard_map/ppermute | solution.py:30
  37.0 1.7 collective-permute-start.20
  38.6 3.9 %collective-permute-done.20 = f32[40,256]{1,0:T(8,128)} collective-permute-done((f32[40,256]{1,0:T(8,128)S(1)}, f32[40,256]{1,0:T(8,128)}, u32[]{:S(2)}, u32[]{:S(2)}) %collective-permute-start.20) | collective-permute-done | bytes 40992 | tf_op jit(solution)/shard_map/ppermute | solution.py:30
  43.6 2.9 %constant_dynamic-slice_fusion.5 = (bf16[256,1024]{1,0:T(8,128)(2,1)}, bf16[256,1024]{1,0:T(8,128)(2,1)}, bf16[256,1024]{1,0:T(8,128)(2,1)}, bf16[256,1024]{1,0:T(8,128)(2,1)}) fusion(bf16[256,4096]{1,0:T(8,128)(2,1)} %param.12, s32[]{:T(128)S(6)} %select_n.46, s32[]{:T(128)S(6)} %select_n.44, s32[]{:T(128)S(6)} %select_n.43, s32[]{:T(128)S(6)} %select_n.45), kind=kLoop, calls=%fused_computation.39 | loop fusion | bytes 4194320 | tf_op jit(solution)/shard_map/dynamic_slice | solution.py:318
  46.5 1.7 collective-permute-start.4
  48.2 1.0 collective-permute-start.5
  51.4 2.9 %collective-permute-start.1 = (bf16[256,1024]{1,0:T(8,128)(2,1)}, bf16[256,1024]{1,0:T(8,128)(2,1)}, u32[]{:S(2)}, u32[]{:S(2)}) collective-permute-start(bf16[256,1024]{1,0:T(8,128)(2,1)} %get-tuple-element.38), channel_id=1, source_target_pairs={{0,2},{1,3},{2,0},{3,1},{4,6},{5,7},{6,4},{7,5},{8,10},{9,11},{10,... | collective-permute-start | bytes 1572872 | tf_op jit(solution)/shard_map/ppermute | solution.py:30
  55.0 1.0 collective-permute-start.2
  56.5 18.2 %turn.1 = bf16[2,32,64,256]{3,2,1,0:T(8,128)(2,1)} custom-call(s32[32]{0:T(128)} %broadcast_xor_fusion.order_ref, s32[1]{0:T(128)} %bitcast.1.core_ref, bf16[256,4096]{1,0:T(8,128)(2,1)} %hidden_ref.3), custom_call_target="tpu_custom_call" | custom-call | flops 1000 | bytes 4200000 | tf_op jit(solution)/shard_map/turn/pallas_call | solution.py:104
  76.9 0.9 copy-done.6
  77.9 0.9 copy-done.8
  79.8 5.0 %project.1 = (bf16[4096,256]{1,0:T(8,128)(2,1)S(1)}, bf16[256,256]{1,0:T(8,128)(2,1)S(1)}) custom-call(s32[32]{0:T(128)S(1)} %copy-done.14, s32[1]{0:T(128)} %bitcast.1.core_ref, bf16[256,4096]{1,0:T(8,128)(2,1)S(1)} %copy-done, bf16[8,64,256]{2,1,0:T(8,128)(2,1)S(1)} %pad_maximum_fusion.refs_0_, bf16[8,64,256]{2,1,0:T(8,128)(2,1)S(1)} %collective-permute-done.9.refs_1_, ...), custom_call_target="tpu_custom_call" | custom-call | flops 540000000 | bytes 6000000 | tf_op jit(solution)/shard_map/project/pallas_call | solution.py:139
  84.8 1.3 copy-done.3
  86.1 3.7 %collective-permute-start.17 = (bf16[256,256]{1,0:T(8,128)(2,1)S(1)}, bf16[256,256]{1,0:T(8,128)(2,1)S(1)}, u32[]{:S(2)}, u32[]{:S(2)}) collective-permute-start(bf16[256,256]{1,0:T(8,128)(2,1)S(1)} %get-tuple-element.16.refs_8_), channel_id=1, source_target_pairs={{0,2},{1,3},{2,0},{3,1},{4,6},{5,7},{6,4},{7,5},{8,10},{9,11},{10,... | collective-permute-start | bytes 393224 | tf_op jit(solution)/shard_map/ppermute | solution.py:30
  89.8 1.0 collective-permute-start.18
  91.5 1.0 div.46.refs_15_
  94.3 8.2 %decays.1 = (bf16[4,16,256,256]{3,2,1,0:T(8,128)(2,1)}, f32[4,256,1024]{2,1,0:T(8,128)S(1)}, f32[4,256,1024]{2,1,0:T(8,128)S(1)}) custom-call(f32[4,40,256]{2,1,0:T(8,128)S(1)} %copy-done.12), custom_call_target="tpu_custom_call" | custom-call | flops 40000000 | bytes 17000000 | tf_op jit(solution)/shard_map/decays/pallas_call | solution.py:80
  102.5 2.1 copy-done.1
  104.6 1.9 copy-done.2
  107.4 24.8 %layer.1 = (bf16[256,1024]{1,0:T(8,128)(2,1)}, bf16[256,1024]{1,0:T(8,128)(2,1)}, bf16[256,1024]{1,0:T(8,128)(2,1)}, bf16[256,1024]{1,0:T(8,128)(2,1)}, f32[256,...) custom-call(s32[1]{0:T(128)} %bitcast.place_ref, ...), custom_call_target="tpu_custom_call" | custom-call | flops 5000000000 | bytes 24000000 | tf_op jit(solution)/shard_map/layer/pallas_call | solution.py:235
  132.3 3.7 %collective-permute-start.26 = (bf16[256,256]{1,0:T(8,128)(2,1)}, bf16[256,256]{1,0:T(8,128)(2,1)S(1)}, u32[]{:S(2)}, u32[]{:S(2)}) collective-permute-start(bf16[256,256]{1,0:T(8,128)(2,1)} %get-tuple-element.26), channel_id=1, source_target_pairs={{0,2},{1,3},{2,0},{3,1},{4,6},{5,7},{6,4},{7,5},{8,10},{9,11},{10,... | collective-permute-start | bytes 393224 | tf_op jit(solution)/shard_map/ppermute | solution.py:30
  136.0 1.0 collective-permute-start.27
  137.5 3.1 %collective-permute-done.26 = bf16[256,256]{1,0:T(8,128)(2,1)S(1)} collective-permute-done((bf16[256,256]{1,0:T(8,128)(2,1)}, bf16[256,256]{1,0:T(8,128)(2,1)S(1)}, u32[]{:S(2)}, u32[]{:S(2)}) %collective-permute-start.26) | collective-permute-done | bytes 131104 | tf_op jit(solution)/shard_map/ppermute | solution.py:30
  140.6 1.8 collective-permute-done.27
  143.0 2.6 collective-permute-done.28
  146.2 1.8 collective-permute-start.29
  148.0 1.7 collective-permute-start.30
  150.2 5.2 %collective-permute-done.29 = bf16[8,64,256]{2,1,0:T(8,128)(2,1)S(1)} collective-permute-done((bf16[8,64,256]{2,1,0:T(8,128)(2,1)S(1)}, bf16[8,64,256]{2,1,0:T(8,128)(2,1)S(1)}, u32[]{:S(2)}, u32[]{:S(2)}) %collective-permute-start.29) | collective-permute-done | bytes 262176 | tf_op jit(solution)/shard_map/ppermute | solution.py:26
  155.4 6.5 %collective-permute-done.30 = bf16[8,64,256]{2,1,0:T(8,128)(2,1)S(1)} collective-permute-done((bf16[8,64,256]{2,1,0:T(8,128)(2,1)S(1)}, bf16[8,64,256]{2,1,0:T(8,128)(2,1)S(1)}, u32[]{:S(2)}, u32[]{:S(2)}) %collective-permute-start.30) | collective-permute-done | bytes 262176 | tf_op jit(solution)/shard_map/ppermute | solution.py:26
  161.9 1.5 collective-permute-done.31
  164.0 4.6 %collective-permute-done.32 = bf16[4,64,256]{2,1,0:T(8,128)(2,1)S(1)} collective-permute-done((bf16[4,64,256]{2,1,0:T(8,128)(2,1)S(1)}, bf16[4,64,256]{2,1,0:T(8,128)(2,1)S(1)}, u32[]{:S(2)}, u32[]{:S(2)}) %collective-permute-start.32) | collective-permute-done | bytes 131104 | tf_op jit(solution)/shard_map/ppermute | solution.py:26
  168.6 1.0 collective-permute-start.33
  169.6 4.8 %collective-permute-done.33 = bf16[2,64,256]{2,1,0:T(8,128)(2,1)S(1)} collective-permute-done((bf16[2,64,256]{2,1,0:T(8,128)(2,1)S(1)}, bf16[2,64,256]{2,1,0:T(8,128)(2,1)S(1)}, u32[]{:S(2)}, u32[]{:S(2)}) %collective-permute-start.33) | collective-permute-done | bytes 65568 | tf_op jit(solution)/shard_map/ppermute | solution.py:26
  174.4 4.5 %collective-permute-start.34 = (bf16[1,64,256]{2,1,0:T(8,128)(2,1)S(1)}, bf16[1,64,256]{2,1,0:T(8,128)(2,1)S(1)}, u32[]{:S(2)}, u32[]{:S(2)}) collective-permute-start(bf16[1,64,256]{2,1,0:T(8,128)(2,1)S(1)} %slice.95), channel_id=1, source_target_pairs={{0,128},{4,132},{8,136},{12,140},{16,144},{20,148},{24,152},{28,15... | collective-permute-start | bytes 98312 | tf_op jit(solution)/shard_map/ppermute | solution.py:26
  179.0 2.2 collective-permute-start.23
  181.2 2.5 collective-permute-start.24
  183.8 18.8 %collective-permute-done.35 = f32[64,256]{1,0:T(8,128)S(1)} collective-permute-done((f32[64,256]{1,0:T(8,128)S(1)}, f32[64,256]{1,0:T(8,128)S(1)}, u32[]{:S(2)}, u32[]{:S(2)}) %collective-permute-start.35) | collective-permute-done | bytes 65568 | tf_op jit(solution)/shard_map/ppermute | solution.py:30
  202.7 2.1 convolution_convert_fusion
  206.0 64.7 %gather_heads.1 = bf16[256,4096]{1,0:T(8,128)(2,1)} custom-call(s32[1]{0:T(128)} %bitcast.place_ref, bf16[256,1024]{1,0:T(8,128)(2,1)} %get-tuple-element.20.p0, bf16[256,1024]{1,0:T(8,128)(2,1)} %copy-done.17, bf16[256,1024]{1,0:T(8,128)(2,1)} %copy-done.18, bf16[256,1024]{1,0:T(8,128)(2,1)} %copy-done.19), custom_call_target="tpu_custom_call" | custom-call | tf_op jit(solution)/shard_map/gather_heads/pallas_call | solution.py:279
  (148 shorter events, 18.6 us)
Async XLA Ops:
  0.6 11.7 %collective-permute-start.6 = (bf16[1,64,256]{2,1,0:T(8,128)(2,1)}, bf16[1,64,256]{2,1,0:T(8,128)(2,1)S(1)}, u32[]{:S(2)}, u32[]{:S(2)}) collective-permute-start(bf16[1,64,256]{2,1,0:T(8,128)(2,1)} %bitcast.33), channel_id=1, source_target_pairs={{0,128},{4,132},{8,136},{12,140},{16,144},{20,148},{24,152},{28,15... | collective-permute-start | bytes 98312 | tf_op jit(solution)/shard_map/ppermute | solution.py:26
  10.8 37.4 %collective-permute-start.3 = (bf16[256,1024]{1,0:T(8,128)(2,1)S(1)}, bf16[256,1024]{1,0:T(8,128)(2,1)S(1)}, u32[]{:S(2)}, u32[]{:S(2)}) collective-permute-start(bf16[256,1024]{1,0:T(8,128)(2,1)S(1)} %get-tuple-element.32), channel_id=1, source_target_pairs={{0,1},{1,0},{2,3},{3,2},{4,5},{5,4},{6,7},{7,6},{8,9},{9,8},{10,11... | collective-permute-start | bytes 1572872 | tf_op jit(solution)/shard_map/ppermute | solution.py:30
  12.4 6.0 %collective-permute-start.7 = (bf16[2,64,256]{2,1,0:T(8,128)(2,1)S(1)}, bf16[2,64,256]{2,1,0:T(8,128)(2,1)S(1)}, u32[]{:S(2)}, u32[]{:S(2)}) collective-permute-start(bf16[2,64,256]{2,1,0:T(8,128)(2,1)S(1)} %pad_maximum_fusion.4), channel_id=1, source_target_pairs={{0,64},{4,68},{8,72},{12,76},{16,80},{20,84},{24,88},{28,92},{32,9... | collective-permute-start | bytes 196616 | tf_op jit(solution)/shard_map/ppermute | solution.py:26
  18.4 5.1 %collective-permute-start.8 = (bf16[4,64,256]{2,1,0:T(8,128)(2,1)S(1)}, bf16[4,64,256]{2,1,0:T(8,128)(2,1)S(1)}, u32[]{:S(2)}, u32[]{:S(2)}) collective-permute-start(bf16[4,64,256]{2,1,0:T(8,128)(2,1)S(1)} %pad_maximum_fusion.3), channel_id=1, source_target_pairs={{0,32},{4,36},{8,40},{12,44},{16,48},{20,52},{24,56},{28,60},{32,0... | collective-permute-start | bytes 393224 | tf_op jit(solution)/shard_map/ppermute | solution.py:26
  23.5 19.1 %collective-permute-start.9 = (bf16[8,64,256]{2,1,0:T(8,128)(2,1)S(1)}, bf16[8,64,256]{2,1,0:T(8,128)(2,1)S(1)}, u32[]{:S(2)}, u32[]{:S(2)}) collective-permute-start(bf16[8,64,256]{2,1,0:T(8,128)(2,1)S(1)} %pad_maximum_fusion.refs_0_), channel_id=1, source_target_pairs={{0,8},{4,12},{8,0},{12,4},{16,24},{20,28},{24,16},{28,20},{32,40},... | collective-permute-start | bytes 786440 | tf_op jit(solution)/shard_map/ppermute | solution.py:26
  24.1 19.0 %collective-permute-start.10 = (bf16[8,64,256]{2,1,0:T(8,128)(2,1)S(1)}, bf16[8,64,256]{2,1,0:T(8,128)(2,1)S(1)}, u32[]{:S(2)}, u32[]{:S(2)}) collective-permute-start(bf16[8,64,256]{2,1,0:T(8,128)(2,1)S(1)} %pad_maximum_fusion.refs_0_), channel_id=1, source_target_pairs={{0,16},{4,20},{8,24},{12,28},{16,0},{20,4},{24,8},{28,12},{32,48},... | collective-permute-start | bytes 786440 | tf_op jit(solution)/shard_map/ppermute | solution.py:26
  26.5 16.7 %collective-permute-start.11 = (bf16[8,64,256]{2,1,0:T(8,128)(2,1)S(1)}, bf16[8,64,256]{2,1,0:T(8,128)(2,1)S(1)}, u32[]{:S(2)}, u32[]{:S(2)}) collective-permute-start(bf16[8,64,256]{2,1,0:T(8,128)(2,1)S(1)} %pad_maximum_fusion.refs_0_), channel_id=1, source_target_pairs={{0,24},{4,28},{8,16},{12,20},{16,8},{20,12},{24,0},{28,4},{32,56},... | collective-permute-start | bytes 786440 | tf_op jit(solution)/shard_map/ppermute | solution.py:26
  27.7 5.2 %collective-permute-start.21 = (f32[40,256]{1,0:T(8,128)S(1)}, f32[40,256]{1,0:T(8,128)S(1)}, u32[]{:S(2)}, u32[]{:S(2)}) collective-permute-start(f32[40,256]{1,0:T(8,128)S(1)} %get-tuple-element.43), channel_id=1, source_target_pairs={{0,3},{1,2},{2,1},{3,0},{4,7},{5,6},{6,5},{7,4},{8,11},{9,10},{10,... | collective-permute-start | bytes 122888 | tf_op jit(solution)/shard_map/ppermute | solution.py:30
  32.9 4.0 %collective-permute-start.19 = (f32[40,256]{1,0:T(8,128)S(1)}, f32[40,256]{1,0:T(8,128)S(1)}, u32[]{:S(2)}, u32[]{:S(2)}) collective-permute-start(f32[40,256]{1,0:T(8,128)S(1)} %get-tuple-element.45), channel_id=1, source_target_pairs={{0,1},{1,0},{2,3},{3,2},{4,5},{5,4},{6,7},{7,6},{8,9},{9,8},{10,11... | collective-permute-start | bytes 122888 | tf_op jit(solution)/shard_map/ppermute | solution.py:30
  36.9 19.1 %copy-start.38 = (s32[32]{0:T(128)S(1)}, s32[32]{0:T(128)}, u32[]{:S(2)}) copy-start(s32[32]{0:T(128)} %constant.78.clone) | copy-start | bytes 388
  37.0 5.6 %collective-permute-start.20 = (f32[40,256]{1,0:T(8,128)S(1)}, f32[40,256]{1,0:T(8,128)}, u32[]{:S(2)}, u32[]{:S(2)}) collective-permute-start(f32[40,256]{1,0:T(8,128)S(1)} %get-tuple-element.44), channel_id=1, source_target_pairs={{0,2},{1,3},{2,0},{3,1},{4,6},{5,7},{6,4},{7,5},{8,10},{9,11},{10,... | collective-permute-start | bytes 122888 | tf_op jit(solution)/shard_map/ppermute | solution.py:30
  42.6 3.9 %collective-permute-start.12 = (bf16[8,64,256]{2,1,0:T(8,128)(2,1)S(1)}, bf16[8,64,256]{2,1,0:T(8,128)(2,1)S(1)}, u32[]{:S(2)}, u32[]{:S(2)}) collective-permute-start(bf16[8,64,256]{2,1,0:T(8,128)(2,1)S(1)} %pad_maximum_fusion.refs_0_), channel_id=1, source_target_pairs={{0,4},{4,0},{8,12},{12,8},{16,20},{20,16},{24,28},{28,24},{32,36},... | collective-permute-start | bytes 786440 | tf_op jit(solution)/shard_map/ppermute | solution.py:26
  42.6 6.6 %collective-permute-start.13 = (bf16[8,64,256]{2,1,0:T(8,128)(2,1)S(1)}, bf16[8,64,256]{2,1,0:T(8,128)(2,1)S(1)}, u32[]{:S(2)}, u32[]{:S(2)}) collective-permute-start(bf16[8,64,256]{2,1,0:T(8,128)(2,1)S(1)} %collective-permute-done.9.refs_1_), channel_id=1, source_target_pairs={{0,4},{4,0},{8,12},{12,8},{16,20},{20,16},{24,28},{28,24},{32,36},... | collective-permute-start | bytes 786440 | tf_op jit(solution)/shard_map/ppermute | solution.py:26
  43.1 7.6 %collective-permute-start.14 = (bf16[8,64,256]{2,1,0:T(8,128)(2,1)S(1)}, bf16[8,64,256]{2,1,0:T(8,128)(2,1)S(1)}, u32[]{:S(2)}, u32[]{:S(2)}) collective-permute-start(bf16[8,64,256]{2,1,0:T(8,128)(2,1)S(1)} %collective-permute-done.10.refs_2_), channel_id=1, source_target_pairs={{0,4},{4,0},{8,12},{12,8},{16,20},{20,16},{24,28},{28,24},{32,36},... | collective-permute-start | bytes 786440 | tf_op jit(solution)/shard_map/ppermute | solution.py:26
  43.2 11.1 %collective-permute-start.15 = (bf16[8,64,256]{2,1,0:T(8,128)(2,1)S(1)}, bf16[8,64,256]{2,1,0:T(8,128)(2,1)S(1)}, u32[]{:S(2)}, u32[]{:S(2)}) collective-permute-start(bf16[8,64,256]{2,1,0:T(8,128)(2,1)S(1)} %collective-permute-done.11.refs_3_), channel_id=1, source_target_pairs={{0,4},{4,0},{8,12},{12,8},{16,20},{20,16},{24,28},{28,24},{32,36},... | collective-permute-start | bytes 786440 | tf_op jit(solution)/shard_map/ppermute | solution.py:26
  46.5 39.6 %collective-permute-start.4 = (bf16[256,1024]{1,0:T(8,128)(2,1)}, bf16[256,1024]{1,0:T(8,128)(2,1)}, u32[]{:S(2)}, u32[]{:S(2)}) collective-permute-start(bf16[256,1024]{1,0:T(8,128)(2,1)} %get-tuple-element.34), channel_id=1, source_target_pairs={{0,2},{1,3},{2,0},{3,1},{4,6},{5,7},{6,4},{7,5},{8,10},{9,11},{10,... | collective-permute-start | bytes 1572872 | tf_op jit(solution)/shard_map/ppermute | solution.py:30
  48.2 37.9 %collective-permute-start.5 = (bf16[256,1024]{1,0:T(8,128)(2,1)}, bf16[256,1024]{1,0:T(8,128)(2,1)}, u32[]{:S(2)}, u32[]{:S(2)}) collective-permute-start(bf16[256,1024]{1,0:T(8,128)(2,1)} %get-tuple-element.31), channel_id=1, source_target_pairs={{0,3},{1,2},{2,1},{3,0},{4,7},{5,6},{6,5},{7,4},{8,11},{9,10},{10,... | collective-permute-start | bytes 1572872 | tf_op jit(solution)/shard_map/ppermute | solution.py:30
  49.8 39.9 %collective-permute-start = (bf16[256,1024]{1,0:T(8,128)(2,1)}, bf16[256,1024]{1,0:T(8,128)(2,1)}, u32[]{:S(2)}, u32[]{:S(2)}) collective-permute-start(bf16[256,1024]{1,0:T(8,128)(2,1)} %get-tuple-element.36), channel_id=1, source_target_pairs={{0,1},{1,0},{2,3},{3,2},{4,5},{5,4},{6,7},{7,6},{8,9},{9,8},{10,11... | collective-permute-start | bytes 1572872 | tf_op jit(solution)/shard_map/ppermute | solution.py:30
  51.4 55.2 %collective-permute-start.1 = (bf16[256,1024]{1,0:T(8,128)(2,1)}, bf16[256,1024]{1,0:T(8,128)(2,1)}, u32[]{:S(2)}, u32[]{:S(2)}) collective-permute-start(bf16[256,1024]{1,0:T(8,128)(2,1)} %get-tuple-element.38), channel_id=1, source_target_pairs={{0,2},{1,3},{2,0},{3,1},{4,6},{5,7},{6,4},{7,5},{8,10},{9,11},{10,... | collective-permute-start | bytes 1572872 | tf_op jit(solution)/shard_map/ppermute | solution.py:30
  55.0 51.6 %collective-permute-start.2 = (bf16[256,1024]{1,0:T(8,128)(2,1)}, bf16[256,1024]{1,0:T(8,128)(2,1)}, u32[]{:S(2)}, u32[]{:S(2)}) collective-permute-start(bf16[256,1024]{1,0:T(8,128)(2,1)} %get-tuple-element.35), channel_id=1, source_target_pairs={{0,3},{1,2},{2,1},{3,0},{4,7},{5,6},{6,5},{7,4},{8,11},{9,10},{10,... | collective-permute-start | bytes 1572872 | tf_op jit(solution)/shard_map/ppermute | solution.py:30
  56.5 19.0 %copy-start.22 = (f32[1,40,256]{2,1,0:T(8,128)S(1)}, f32[1,40,256]{2,1,0:T(8,128)}, u32[]{:S(2)}) copy-start(f32[1,40,256]{2,1,0:T(8,128)} %get-tuple-element.42) | copy-start | bytes 122884
  56.5 19.0 %copy-start.28 = (f32[40,256]{1,0:T(8,128)S(1)}, f32[40,256]{1,0:T(8,128)}, u32[]{:S(2)}) copy-start(f32[40,256]{1,0:T(8,128)} %copy-done.27) | copy-start | bytes 122884
  56.5 19.0 %copy-start.30 = (f32[40,256]{1,0:T(8,128)S(1)}, f32[40,256]{1,0:T(8,128)}, u32[]{:S(2)}) copy-start(f32[40,256]{1,0:T(8,128)} %copy-done.29) | copy-start | bytes 122884
  56.5 20.4 %copy-start = (bf16[256,4096]{1,0:T(8,128)(2,1)S(1)}, bf16[256,4096]{1,0:T(8,128)(2,1)}, u32[]{:S(2)}) copy-start(bf16[256,4096]{1,0:T(8,128)(2,1)} %hidden_ref.3) | copy-start | bytes 6291460
  56.5 20.4 %copy-start.14 = (s32[32]{0:T(128)S(1)}, s32[32]{0:T(128)}, u32[]{:S(2)}) copy-start(s32[32]{0:T(128)} %broadcast_xor_fusion.order_ref) | copy-start | bytes 388
  86.1 20.5 %collective-permute-start.16 = (bf16[256,256]{1,0:T(8,128)(2,1)S(1)}, bf16[256,256]{1,0:T(8,128)(2,1)S(1)}, u32[]{:S(2)}, u32[]{:S(2)}) collective-permute-start(bf16[256,256]{1,0:T(8,128)(2,1)S(1)} %get-tuple-element.16.refs_8_), channel_id=1, source_target_pairs={{0,1},{1,0},{2,3},{3,2},{4,5},{5,4},{6,7},{7,6},{8,9},{9,8},{10,11... | collective-permute-start | bytes 393224 | tf_op jit(solution)/shard_map/ppermute | solution.py:30
  86.1 20.5 %collective-permute-start.17 = (bf16[256,256]{1,0:T(8,128)(2,1)S(1)}, bf16[256,256]{1,0:T(8,128)(2,1)S(1)}, u32[]{:S(2)}, u32[]{:S(2)}) collective-permute-start(bf16[256,256]{1,0:T(8,128)(2,1)S(1)} %get-tuple-element.16.refs_8_), channel_id=1, source_target_pairs={{0,2},{1,3},{2,0},{3,1},{4,6},{5,7},{6,4},{7,5},{8,10},{9,11},{10,... | collective-permute-start | bytes 393224 | tf_op jit(solution)/shard_map/ppermute | solution.py:30
  89.8 16.8 %collective-permute-start.18 = (bf16[256,256]{1,0:T(8,128)(2,1)S(1)}, bf16[256,256]{1,0:T(8,128)(2,1)S(1)}, u32[]{:S(2)}, u32[]{:S(2)}) collective-permute-start(bf16[256,256]{1,0:T(8,128)(2,1)S(1)} %get-tuple-element.16.refs_8_), channel_id=1, source_target_pairs={{0,3},{1,2},{2,1},{3,0},{4,7},{5,6},{6,5},{7,4},{8,11},{9,10},{10,... | collective-permute-start | bytes 393224 | tf_op jit(solution)/shard_map/ppermute | solution.py:30
  107.4 29.6 %copy-start.15 = (bf16[2,32,64,256]{3,2,1,0:T(8,128)(2,1)S(1)}, bf16[2,32,64,256]{3,2,1,0:T(8,128)(2,1)}, u32[]{:S(2)}) copy-start(bf16[2,32,64,256]{3,2,1,0:T(8,128)(2,1)} %turn.1) | copy-start | bytes 6291460
  132.2 5.3 %collective-permute-start.25 = (bf16[256,256]{1,0:T(8,128)(2,1)}, bf16[256,256]{1,0:T(8,128)(2,1)S(1)}, u32[]{:S(2)}, u32[]{:S(2)}) collective-permute-start(bf16[256,256]{1,0:T(8,128)(2,1)} %get-tuple-element.25), channel_id=1, source_target_pairs={{0,1},{1,0},{2,3},{3,2},{4,5},{5,4},{6,7},{7,6},{8,9},{9,8},{10,11... | collective-permute-start | bytes 393224 | tf_op jit(solution)/shard_map/ppermute | solution.py:30
  132.3 8.3 %collective-permute-start.26 = (bf16[256,256]{1,0:T(8,128)(2,1)}, bf16[256,256]{1,0:T(8,128)(2,1)S(1)}, u32[]{:S(2)}, u32[]{:S(2)}) collective-permute-start(bf16[256,256]{1,0:T(8,128)(2,1)} %get-tuple-element.26), channel_id=1, source_target_pairs={{0,2},{1,3},{2,0},{3,1},{4,6},{5,7},{6,4},{7,5},{8,10},{9,11},{10,... | collective-permute-start | bytes 393224 | tf_op jit(solution)/shard_map/ppermute | solution.py:30
  136.0 6.4 %collective-permute-start.27 = (bf16[256,256]{1,0:T(8,128)(2,1)}, bf16[256,256]{1,0:T(8,128)(2,1)S(1)}, u32[]{:S(2)}, u32[]{:S(2)}) collective-permute-start(bf16[256,256]{1,0:T(8,128)(2,1)} %get-tuple-element.27), channel_id=1, source_target_pairs={{0,3},{1,2},{2,1},{3,0},{4,7},{5,6},{6,5},{7,4},{8,11},{9,10},{10,... | collective-permute-start | bytes 393224 | tf_op jit(solution)/shard_map/ppermute | solution.py:30
  142.9 2.7 %collective-permute-start.28 = (bf16[2048,256]{1,0:T(8,128)(2,1)S(1)}, bf16[2048,256]{1,0:T(8,128)(2,1)S(1)}, u32[]{:S(2)}, u32[]{:S(2)}) collective-permute-start(bf16[2048,256]{1,0:T(8,128)(2,1)S(1)} %convolution_convert_fusion.1), channel_id=1, source_target_pairs={{0,4},{4,0},{8,12},{12,8},{16,20},{20,16},{24,28},{28,24},{32,36},... | collective-permute-start | bytes 3145736 | tf_op jit(solution)/shard_map/ppermute | solution.py:26
  146.2 9.2 %collective-permute-start.29 = (bf16[8,64,256]{2,1,0:T(8,128)(2,1)S(1)}, bf16[8,64,256]{2,1,0:T(8,128)(2,1)S(1)}, u32[]{:S(2)}, u32[]{:S(2)}) collective-permute-start(bf16[8,64,256]{2,1,0:T(8,128)(2,1)S(1)} %bitcast.40), channel_id=1, source_target_pairs={{0,8},{4,12},{8,0},{12,4},{16,24},{20,28},{24,16},{28,20},{32,40},... | collective-permute-start | bytes 786440 | tf_op jit(solution)/shard_map/ppermute | solution.py:26
  148.0 13.9 %collective-permute-start.30 = (bf16[8,64,256]{2,1,0:T(8,128)(2,1)S(1)}, bf16[8,64,256]{2,1,0:T(8,128)(2,1)S(1)}, u32[]{:S(2)}, u32[]{:S(2)}) collective-permute-start(bf16[8,64,256]{2,1,0:T(8,128)(2,1)S(1)} %bitcast.39), channel_id=1, source_target_pairs={{0,16},{4,20},{8,24},{12,28},{16,0},{20,4},{24,8},{28,12},{32,48},... | collective-permute-start | bytes 786440 | tf_op jit(solution)/shard_map/ppermute | solution.py:26
  149.7 13.7 %collective-permute-start.31 = (bf16[8,64,256]{2,1,0:T(8,128)(2,1)S(1)}, bf16[8,64,256]{2,1,0:T(8,128)(2,1)S(1)}, u32[]{:S(2)}, u32[]{:S(2)}) collective-permute-start(bf16[8,64,256]{2,1,0:T(8,128)(2,1)S(1)} %bitcast.38), channel_id=1, source_target_pairs={{0,24},{4,28},{8,16},{12,20},{16,8},{20,12},{24,0},{28,4},{32,56},... | collective-permute-start | bytes 786440 | tf_op jit(solution)/shard_map/ppermute | solution.py:26
  150.2 28.8 %copy-start.35 = (bf16[256,1024]{1,0:T(8,128)(2,1)S(1)}, bf16[256,1024]{1,0:T(8,128)(2,1)}, u32[]{:S(2)}) copy-start(bf16[256,1024]{1,0:T(8,128)(2,1)} %get-tuple-element.21) | copy-start | bytes 1572868
  150.2 28.8 %copy-start.34 = (bf16[256,1024]{1,0:T(8,128)(2,1)S(1)}, bf16[256,1024]{1,0:T(8,128)(2,1)}, u32[]{:S(2)}) copy-start(bf16[256,1024]{1,0:T(8,128)(2,1)} %get-tuple-element.22) | copy-start | bytes 1572868
  150.2 31.1 %copy-start.33 = (bf16[256,1024]{1,0:T(8,128)(2,1)S(1)}, bf16[256,1024]{1,0:T(8,128)(2,1)}, u32[]{:S(2)}) copy-start(bf16[256,1024]{1,0:T(8,128)(2,1)} %get-tuple-element.23) | copy-start | bytes 1572868
  150.2 52.6 %copy-start.4 = (bf16[4096,256]{1,0:T(8,128)(2,1)S(1)}, bf16[4096,256]{1,0:T(8,128)(2,1)}, u32[]{:S(2)}) copy-start(bf16[4096,256]{1,0:T(8,128)(2,1)} %copy-done.3) | copy-start | bytes 6291460
  163.5 5.1 %collective-permute-start.32 = (bf16[4,64,256]{2,1,0:T(8,128)(2,1)S(1)}, bf16[4,64,256]{2,1,0:T(8,128)(2,1)S(1)}, u32[]{:S(2)}, u32[]{:S(2)}) collective-permute-start(bf16[4,64,256]{2,1,0:T(8,128)(2,1)S(1)} %slice.93), channel_id=1, source_target_pairs={{0,32},{4,36},{8,40},{12,44},{16,48},{20,52},{24,56},{28,60},{32,0... | collective-permute-start | bytes 393224 | tf_op jit(solution)/shard_map/ppermute | solution.py:26
  168.6 5.8 %collective-permute-start.33 = (bf16[2,64,256]{2,1,0:T(8,128)(2,1)S(1)}, bf16[2,64,256]{2,1,0:T(8,128)(2,1)S(1)}, u32[]{:S(2)}, u32[]{:S(2)}) collective-permute-start(bf16[2,64,256]{2,1,0:T(8,128)(2,1)S(1)} %slice.94), channel_id=1, source_target_pairs={{0,64},{4,68},{8,72},{12,76},{16,80},{20,84},{24,88},{28,92},{32,9... | collective-permute-start | bytes 196616 | tf_op jit(solution)/shard_map/ppermute | solution.py:26
  174.4 9.3 %collective-permute-start.34 = (bf16[1,64,256]{2,1,0:T(8,128)(2,1)S(1)}, bf16[1,64,256]{2,1,0:T(8,128)(2,1)S(1)}, u32[]{:S(2)}, u32[]{:S(2)}) collective-permute-start(bf16[1,64,256]{2,1,0:T(8,128)(2,1)S(1)} %slice.95), channel_id=1, source_target_pairs={{0,128},{4,132},{8,136},{12,140},{16,144},{20,148},{24,152},{28,15... | collective-permute-start | bytes 98312 | tf_op jit(solution)/shard_map/ppermute | solution.py:26
  179.0 25.8 %collective-permute-start.22 = (bf16[256,1024]{1,0:T(8,128)(2,1)S(1)}, bf16[256,1024]{1,0:T(8,128)(2,1)S(1)}, u32[]{:S(2)}, u32[]{:S(2)}) collective-permute-start(bf16[256,1024]{1,0:T(8,128)(2,1)S(1)} %copy-done.35), channel_id=1, source_target_pairs={{0,1},{1,0},{2,3},{3,2},{4,5},{5,4},{6,7},{7,6},{8,9},{9,8},{10,11... | collective-permute-start | bytes 1572872 | tf_op jit(solution)/shard_map/ppermute | solution.py:30
  179.0 25.8 %collective-permute-start.23 = (bf16[256,1024]{1,0:T(8,128)(2,1)S(1)}, bf16[256,1024]{1,0:T(8,128)(2,1)S(1)}, u32[]{:S(2)}, u32[]{:S(2)}) collective-permute-start(bf16[256,1024]{1,0:T(8,128)(2,1)S(1)} %copy-done.34), channel_id=1, source_target_pairs={{0,2},{1,3},{2,0},{3,1},{4,6},{5,7},{6,4},{7,5},{8,10},{9,11},{10,... | collective-permute-start | bytes 1572872 | tf_op jit(solution)/shard_map/ppermute | solution.py:30
  181.2 23.6 %collective-permute-start.24 = (bf16[256,1024]{1,0:T(8,128)(2,1)S(1)}, bf16[256,1024]{1,0:T(8,128)(2,1)S(1)}, u32[]{:S(2)}, u32[]{:S(2)}) collective-permute-start(bf16[256,1024]{1,0:T(8,128)(2,1)S(1)} %copy-done.33), channel_id=1, source_target_pairs={{0,3},{1,2},{2,1},{3,0},{4,7},{5,6},{6,5},{7,4},{8,11},{9,10},{10,... | collective-permute-start | bytes 1572872 | tf_op jit(solution)/shard_map/ppermute | solution.py:30
  183.7 18.9 %collective-permute-start.35 = (f32[64,256]{1,0:T(8,128)S(1)}, f32[64,256]{1,0:T(8,128)S(1)}, u32[]{:S(2)}, u32[]{:S(2)}) collective-permute-start(f32[64,256]{1,0:T(8,128)S(1)} %fusion.1), channel_id=1, source_target_pairs={{0,1},{1,0},{2,3},{3,2},{4,5},{5,4},{6,7},{7,6},{8,9},{9,8},{10,11... | collective-permute-start | bytes 196616 | tf_op jit(solution)/shard_map/ppermute | solution.py:30
  202.6 68.0 %collective-permute-start.36 = (f32[64,256]{1,0:T(8,128)S(1)}, f32[64,256]{1,0:T(8,128)S(1)}, u32[]{:S(2)}, u32[]{:S(2)}) collective-permute-start(f32[64,256]{1,0:T(8,128)S(1)} %add.109), channel_id=1, source_target_pairs={{0,2},{1,3},{2,0},{3,1},{4,6},{5,7},{6,4},{7,5},{8,10},{9,11},{10,... | collective-permute-start | bytes 196616 | tf_op jit(solution)/shard_map/ppermute | solution.py:30
  (28 other events, 116.7 us)

commit v2 on v1

--- a/solution.py
+++ b/solution.py
@@ -54,7 +54,20 @@
     return pl.BlockSpec(memory_space=pltpu.SMEM)
 
 
-def decay_kernel(small_ref, grid_ref, lead_ref, write_ref):
+def after(arrays, waits):
+    n = len(arrays)
+    return pl.pallas_call(
+        lambda *refs: None,
+        in_specs=[anywhere()] * (n + len(waits)),
+        out_specs=[anywhere()] * n,
+        out_shape=[jax.ShapeDtypeStruct(a.shape, a.dtype) for a in arrays],
+        input_output_aliases={i: i for i in range(n)},
+        name="after",
+    )(*arrays, *waits)
+
+
+def decay_kernel(small_ref, grid_ref, lead_ref, write_ref, done_ref):
+    done_ref[...] = jnp.zeros_like(done_ref)
     small = small_ref[0]
     cum_rows = small[0:LOCAL_HEADS]
     step_rows = small[LOCAL_HEADS : 2 * LOCAL_HEADS]
@@ -72,7 +85,8 @@
         at = slice(2 * HEAD * p, 2 * HEAD * (p + 1))
         for ref, base in ((lead_ref, LOCAL_HEADS), (write_ref, 2 * LOCAL_HEADS)):
             c = base + 2 * p
-            ref[0, :, at] = jnp.where(first, columns[:, c : c + 1], columns[:, c + 1 : c + 2])
+            both = jnp.where(first, columns[:, c : c + 1], columns[:, c + 1 : c + 2])
+            ref[0, :, at] = both.astype(BF)
 
 
 def decays(small):
@@ -81,47 +95,112 @@
         decay_kernel,
         grid=(PEERS,),
         in_specs=[blk(*small.shape[1:])],
-        out_specs=[blk(LOCAL_HEADS, BLOCK, BLOCK), blk(BLOCK, WIDE), blk(BLOCK, WIDE)],
+        out_specs=[blk(LOCAL_HEADS, BLOCK, BLOCK), blk(BLOCK, WIDE), blk(BLOCK, WIDE), pl.BlockSpec((8, 128), lambda k: (0, 0))],
         out_shape=[
             jax.ShapeDtypeStruct((PEERS, LOCAL_HEADS, BLOCK, BLOCK), BF),
-            jax.ShapeDtypeStruct((PEERS, BLOCK, WIDE), F32),
-            jax.ShapeDtypeStruct((PEERS, BLOCK, WIDE), F32),
+            jax.ShapeDtypeStruct((PEERS, BLOCK, WIDE), BF),
+            jax.ShapeDtypeStruct((PEERS, BLOCK, WIDE), BF),
+            jax.ShapeDtypeStruct((8, 128), F32),
         ],
-        compiler_params=pltpu.CompilerParams(vmem_limit_bytes=40 * MIB),
+        compiler_params=pltpu.CompilerParams(vmem_limit_bytes=16 * MIB),
         cost_estimate=pl.CostEstimate(flops=40_000_000, bytes_accessed=17_000_000, transcendentals=4_300_000),
         name="decays",
     )(small)
 
 
-def turn_kernel(order_ref, core_ref, hidden_ref, out_ref):
+def cut_heads_kernel(place_ref, values_ref, aux_ref, teacher_ref, *refs):
+    v_outs, t_outs, sems = refs[0:3], refs[3:6], refs[6]
+    copies = []
+    for k in (1, 2, 3):
+        to = place_ref[0] ^ k
+        wide = pl.ds(pl.multiple_of(to * WIDE, WIDE), WIDE)
+        thin = pl.ds(pl.multiple_of(to * 128, 128), 128)
+        for n, (src, dst) in enumerate(
+            (
+                (values_ref.at[:, wide], v_outs[k - 1].at[:, pl.ds(0, WIDE)]),
+                (aux_ref.at[:, thin], v_outs[k - 1].at[:, pl.ds(WIDE, 128)]),
+                (teacher_ref.at[:, wide], t_outs[k - 1]),
+            )
+        ):
+            copies.append(pltpu.make_async_copy(src, dst, sems.at[n, k]))
+            copies[-1].start()
+    for c in copies:
+        c.wait()
+
+
+def cut_heads(place, values, aux, teacher):
+    return pl.pallas_call(
+        cut_heads_kernel,
+        in_specs=[smem()] + [anywhere()] * 3,
+        out_specs=[vmem()] * 6,
+        out_shape=[jax.ShapeDtypeStruct((BLOCK, WIDE + 128), BF)] * 3
+        + [jax.ShapeDtypeStruct((BLOCK, WIDE), BF)] * 3,
+        scratch_shapes=[pltpu.SemaphoreType.DMA((3, 4))],
+        cost_estimate=pl.CostEstimate(flops=1000, bytes_accessed=6_400_000, transcendentals=0),
+        name="cut_heads",
+    )(place, values, aux, teacher)
+
+
+def split_hidden_kernel(x_ref, hidden_ref, *refs):
+    outs, done_ref, sems = refs[:4], refs[4], refs[5]
+    done_ref[...] = jnp.zeros_like(done_ref)
+    copies = []
+    for a in range(4):
+        for z in range(8):
+            at = pl.multiple_of((z * 4 + (x_ref[0] ^ a)) * 128, 128)
+            copies.append(
+                pltpu.make_async_copy(
+                    hidden_ref.at[:, pl.ds(at, 128)],
+                    outs[a].at[:, pl.ds(128 * z, 128)],
+                    sems.at[a, z],
+                )
+            )
+            copies[-1].start()
+    for c in copies:
+        c.wait()
+
+
+def split_hidden(x, hidden):
+    return pl.pallas_call(
+        split_hidden_kernel,
+        in_specs=[smem(), anywhere()],
+        out_specs=[vmem()] * 5,
+        out_shape=[jax.ShapeDtypeStruct((BLOCK, 1024), BF)] * 4 + [jax.ShapeDtypeStruct((8, 128), F32)],
+        scratch_shapes=[pltpu.SemaphoreType.DMA((4, 8))],
+        cost_estimate=pl.CostEstimate(flops=1000, bytes_accessed=4_200_000, transcendentals=0),
+        name="split_hidden",
+    )(x, hidden)
+
+
+def turn_kernel(pos_ref, core_ref, p0, p1, p2, p3, out_ref):
     core = core_ref[0]
-    turned = hidden_ref[...].T
-    out_ref[core, 0] = turned[:HEAD]
-    out_ref[1 - core, 0] = turned[HEAD:]
-
-
-def turn(hidden, order, core):
+    for z in range(8):
+        for a, piece in enumerate((p0, p1, p2, p3)):
+            turned = piece[:, 128 * z : 128 * (z + 1)].T
+            at = slice(BLOCK * a, BLOCK * (a + 1))
+            out_ref[core, pos_ref[z], :, at] = turned[:HEAD]
+            out_ref[1 - core, pos_ref[z], :, at] = turned[HEAD:]
+
+
+def turn(pos, core, pieces):
     return pl.pallas_call(
         turn_kernel,
-        grid_spec=pltpu.PrefetchScalarGridSpec(
-            num_scalar_prefetch=2,
-            grid=(32,),
-            in_specs=[pl.BlockSpec((BLOCK, 128), lambda j, order, core: (0, order[j]))],
-            out_specs=pl.BlockSpec((2, 1, 64, BLOCK), lambda j, order, core: (0, j, 0, 0)),
-        ),
-        out_shape=jax.ShapeDtypeStruct((2, 32, 64, BLOCK), BF),
-        cost_estimate=pl.CostEstimate(flops=1000, bytes_accessed=4_200_000, transcendentals=0),
+        in_specs=[smem(), smem()] + [vmem()] * 4,
+        out_specs=vmem(),
+        out_shape=jax.ShapeDtypeStruct((2, 8, 64, 4 * BLOCK), BF),
+        compiler_params=pltpu.CompilerParams(vmem_limit_bytes=14 * MIB),
+        cost_estimate=pl.CostEstimate(flops=1000, bytes_accessed=14_000_000, transcendentals=0),
         name="turn",
-    )(order, core, hidden)
+    )(pos, core, *pieces)
 
 
 def project_kernel(order_ref, core_ref, hidden_ref, *refs):
     own, other = refs[0:4], refs[4:8]
-    weight_ref, rows_ref, sems = refs[8:]
+    weight_ref, rows_ref, sems = refs[-3:]
     core = core_ref[0]
     copies = []
-    for a in range(4):
-        for side, (pieces, place) in enumerate(((own, core), (other, 1 - core))):
+    for side, (pieces, place) in enumerate(((own, core), (other, 1 - core))):
+        for a in range(4):
             for b in range(8):
                 row = pl.multiple_of(order_ref[a * 8 + b] * 128 + place * 64, 64)
                 copies.append(
@@ -135,20 +214,20 @@
     rows_ref[...] = dot_nn(hidden_ref[...], weight_ref[...]).astype(BF)
 
 
-def project(hidden, own, other, order, core):
+def project(hidden, own, other, order, core, waits):
     return pl.pallas_call(
         project_kernel,
-        in_specs=[smem(), smem(), vmem()] + [anywhere()] * 8,
+        in_specs=[smem(), smem(), vmem()] + [anywhere()] * (8 + len(waits)),
         out_specs=[vmem(), vmem()],
         out_shape=[
             jax.ShapeDtypeStruct((4096, 256), BF),
             jax.ShapeDtypeStruct((BLOCK, 256), BF),
         ],
         scratch_shapes=[pltpu.SemaphoreType.DMA((2, 32))],
-        compiler_params=pltpu.CompilerParams(vmem_limit_bytes=32 * MIB),
+        compiler_params=pltpu.CompilerParams(vmem_limit_bytes=14 * MIB),
         cost_estimate=pl.CostEstimate(flops=540_000_000, bytes_accessed=6_000_000, transcendentals=0),
         name="project",
-    )(order, core, hidden, *own, *other)
+    )(order, core, hidden, *own, *other, *waits)
 
 
 def layer_kernel(place_ref, *refs):
@@ -158,16 +237,19 @@
     (x, t, bc, grid, lead, write, entry, pull, scaled, outs, acc, state, base, cross, score, ig, sem_a, sem_g) = refs[26:]
     place = place_ref[0]
     first = []
-    later = []
+    later = [[] for _ in range(PEERS)]
     for k in range(PEERS):
         first.append(pltpu.make_async_copy(bcs_in[k], bc.at[k], sem_a.at[0, k]))
-        first.append(pltpu.make_async_copy(xs_in[k], x.at[k], sem_a.at[1, k]))
+        own = pl.ds(pl.multiple_of(place * WIDE, WIDE), WIDE)
+        x_in = xs_in[k].at[:, own if k == 0 else pl.ds(0, WIDE)]
+        first.append(pltpu.make_async_copy(x_in, x.at[k], sem_a.at[1, k]))
         first.append(pltpu.make_async_copy(write_in.at[k], write.at[k], sem_a.at[2, k]))
     for k in range(PEERS):
-        later.append(pltpu.make_async_copy(ts_in[k], t.at[k], sem_a.at[3, k]))
-        later.append(pltpu.make_async_copy(lead_in.at[k], lead.at[k], sem_a.at[4, k]))
-        later.append(pltpu.make_async_copy(grid_in.at[k], grid.at[k], sem_g.at[k]))
-    for c in first + later:
+        t_in = ts_in[k].at[:, own] if k == 0 else ts_in[k]
+        later[k].append(pltpu.make_async_copy(t_in, t.at[k], sem_a.at[3, k]))
+        later[k].append(pltpu.make_async_copy(lead_in.at[k], lead.at[k], sem_a.at[4, k]))
+        later[k].append(pltpu.make_async_copy(grid_in.at[k], grid.at[k], sem_g.at[k]))
+    for c in first + sum(later, []):
         c.start()
     for c in first:
         c.wait()
@@ -176,20 +258,19 @@
     for j in range(PEERS):
         k = place ^ j
         entry[k] = state[...].astype(BF)
-        scaled[k] = (write[k] * x[k].astype(F32)).astype(BF)
+        scaled[k] = (write[k].astype(F32) * x[k].astype(F32)).astype(BF)
         if j < PEERS - 1:
             state[...] = keep_ref[k] * state[...] + dot_tn(bc[k, :, :STATE], scaled[k])
-    for c in later:
-        c.wait()
-
     low = lax.broadcasted_iota(jnp.int32, (BLOCK, 2 * HEAD), 1) < HEAD
 
     def block(k, carry):
+        for ref, sem in ((t, sem_a.at[3, k]), (lead, sem_a.at[4, k]), (grid, sem_g.at[k])):
+            pltpu.make_async_copy(ref.at[k], ref.at[k], sem).wait()
         b_map = bc[k, :, :STATE]
         c_map = bc[k, :, STATE:]
         cross[...] = dot_nt(c_map, b_map)
         base[...] = (
-            dot_nn(c_map, entry[k]) * lead[k] + skip_ref[...] * x[k].astype(F32) - t[k].astype(F32)
+            dot_nn(c_map, entry[k]) * lead[k].astype(F32) + skip_ref[...] * x[k].astype(F32) - t[k].astype(F32)
         )
         score[...] = jnp.zeros_like(score)
         weight = weight_ref[k]
@@ -209,7 +290,7 @@
             dx = jnp.where(low, dot_tn(m0, og), dot_tn(m1, og))
             ogf = og.astype(F32)
             acc[k, :, at] = dx + skip_ref[:, at] * ogf
-            outs[:, at] = (lead[k, :, at] * ogf).astype(BF)
+            outs[:, at] = (lead[k, :, at].astype(F32) * ogf).astype(BF)
         sg = score[...].astype(BF)
         pull[k] = dot_tn(c_map, outs[...])
         ig[k, :, STATE:] = dot_nt(outs[...], entry[k]) + dot_nn(sg, b_map)
@@ -222,7 +303,7 @@
     for j in reversed(range(PEERS)):
         k = place ^ j
         leave = state[...].astype(BF)
-        acc[k] = acc[k] + write[k] * dot_nn(bc[k, :, :STATE], leave)
+        acc[k] = acc[k] + write[k].astype(F32) * dot_nn(bc[k, :, :STATE], leave)
         ig[k, :, :STATE] += dot_nt(scaled[k], leave)
         if j > 0:
             state[...] = keep_ref[k] * state[...] + pull[k]
@@ -244,8 +325,8 @@
             pltpu.VMEM((PEERS, BLOCK, WIDE), BF),
             pltpu.VMEM((PEERS, BLOCK, 2 * STATE), BF),
             pltpu.VMEM((PEERS, LOCAL_HEADS, BLOCK, BLOCK), BF),
-            pltpu.VMEM((PEERS, BLOCK, WIDE), F32),
-            pltpu.VMEM((PEERS, BLOCK, WIDE), F32),
+            pltpu.VMEM((PEERS, BLOCK, WIDE), BF),
+            pltpu.VMEM((PEERS, BLOCK, WIDE), BF),
             pltpu.VMEM((PEERS, STATE, WIDE), BF),
             pltpu.VMEM((PEERS, STATE, WIDE), F32),
             pltpu.VMEM((PEERS, BLOCK, WIDE), BF),
@@ -279,9 +360,10 @@
     return pl.pallas_call(
         gather_heads_kernel,
         in_specs=[smem()] + [anywhere()] * 4,
-        out_specs=anywhere(),
+        out_specs=vmem(),
         out_shape=jax.ShapeDtypeStruct((BLOCK, 4 * WIDE), BF),
         scratch_shapes=[pltpu.SemaphoreType.DMA((4,))],
+        cost_estimate=pl.CostEstimate(flops=1000, bytes_accessed=4_200_000, transcendentals=0),
         name="gather_heads",
     )(place, *pieces)
 
@@ -304,57 +386,68 @@
     chip = dp // 2
     distance = jnp.array([z * 4 + a for a in range(4) for z in ZREL], jnp.int32)
     order = (chip ^ distance).astype(jnp.int32)
+    x_place = (chip % 4).astype(jnp.int32).reshape(1)
+    turns = jnp.array([ZREL.index(z) for z in range(8)], jnp.int32)
+    pos = turns[jnp.arange(8, dtype=jnp.int32) ^ (chip // 4)]
     doc_len = BLOCK * PEERS
     all_tokens = doc_len * 64
 
-    r = bc_weight[None]
-    for mask in (32, 16, 8):
-        r = jnp.concatenate([r, over_dp(r, mask)], axis=0)
-    own = [r] + [over_dp(r, 2 * a) for a in (1, 2, 3)]
-    other = [over_dp(p, 1) for p in own]
-
-    def exchange(array):
-        cut = [
-            lax.dynamic_slice_in_dim(array, (me ^ k) * WIDE, WIDE, axis=1) for k in range(PEERS)
-        ]
-        return [cut[0]] + [over_seq(cut[k], k) for k in (1, 2, 3)]
-
-    conf_float = confidence.astype(F32)
-    base = jnp.log(0.9995 + 0.0004 * decay_codes.astype(F32) / 15.0)
+    aux = jnp.concatenate(
+        [
+            decay_codes.astype(BF).reshape(BLOCK, PEERS, LOCAL_HEADS),
+            jnp.broadcast_to(resets.astype(BF)[:, None, None], (BLOCK, PEERS, 1)),
+            jnp.broadcast_to(confidence.astype(BF)[:, None, None], (BLOCK, PEERS, 1)),
+            jnp.zeros((BLOCK, PEERS, 128 - LOCAL_HEADS - 2), BF),
+        ],
+        axis=2,
+    ).reshape(BLOCK, PEERS * 128)
+    cut = cut_heads(place, values, aux, teacher)
+    v_cut, t_cut = cut[0:3], cut[3:6]
+    x1, x3 = over_seq(v_cut[0], 1), over_seq(v_cut[2], 3)
+    (far,) = after([v_cut[1]], [x1])
+    xs = [values, x1, over_seq(far, 2), x3]
+    near = after([t_cut[0], t_cut[2]], [x3])
+    ts = [teacher, over_seq(near[0], 1), over_seq(t_cut[1], 2), over_seq(near[1], 3)]
+
+    facts = jnp.stack(
+        [lax.dynamic_slice_in_dim(aux, me * 128, 128, axis=1)] + [x[:, WIDE:] for x in xs[1:]]
+    ).astype(F32)
+    base = jnp.log(0.9995 + 0.0004 * facts[:, :, :LOCAL_HEADS] / 15.0)
+    rates = lax.dynamic_slice_in_dim(head_decay_rates, me * LOCAL_HEADS, LOCAL_HEADS)
     log_decay = (
-        head_decay_rates[None, :] * (1.0 + SPIKE_MULTIPLIER * resets.astype(F32))[:, None] * base
+        rates[None, None, :] * (1.0 + SPIKE_MULTIPLIER * facts[:, :, LOCAL_HEADS, None]) * base
     )
     lower = (
         lax.broadcasted_iota(jnp.int32, (BLOCK, BLOCK), 0)
         >= lax.broadcasted_iota(jnp.int32, (BLOCK, BLOCK), 1)
     ).astype(F32)
-    cum_rows = lax.dot_general(
-        log_decay, lower, (((0,), (1,)), ((), ())), precision=lax.Precision.HIGHEST
+    cum_rows = jnp.swapaxes(
+        jnp.einsum("ts,ksh->kth", lower, log_decay, precision=lax.Precision.HIGHEST), 1, 2
     )
-    step_rows = (-STEP_FACTOR * base).T
-    packed = jnp.concatenate(
-        [
-            cum_rows.reshape(PEERS, LOCAL_HEADS, BLOCK),
-            step_rows.reshape(PEERS, LOCAL_HEADS, BLOCK),
-            jnp.broadcast_to(conf_float[None, None, :], (PEERS, 8, BLOCK)),
-        ],
-        axis=1,
-    )
-    cut = [lax.dynamic_index_in_dim(packed, me ^ k, 0, keepdims=False) for k in range(PEERS)]
-    small = jnp.stack([cut[0]] + [over_seq(cut[k], k) for k in (1, 2, 3)])
-    grid, lead, write = decays(small)
-    conf_all = small[:, 2 * LOCAL_HEADS]
+    step_rows = jnp.swapaxes(-STEP_FACTOR * base, 1, 2)
+    small = jnp.concatenate([cum_rows, step_rows], axis=1)
+    grid, lead, write, decayed = decays(small)
+    conf_all = facts[:, :, LOCAL_HEADS + 1]
     weight = (conf_all * doc_len / jnp.sum(conf_all))[:, :, None]
     keep = jnp.repeat(jnp.exp(small[:, :LOCAL_HEADS, BLOCK - 1]), HEAD, axis=1)[:, None, :]
     skip = jnp.repeat(
         lax.dynamic_slice_in_dim(skip_gain, me * LOCAL_HEADS, LOCAL_HEADS), HEAD
     )[None, :]
 
-    xs = exchange(values)
-    ts = exchange(teacher)
-    turned = turn(hidden_in, order, core)
-    full_weight, rows = project(hidden_in, own, other, order, core)
+    r = bc_weight[None]
+    r = jnp.concatenate([r, over_dp(r, 32)], axis=0)
+    r = jnp.concatenate([r] + [over_dp(r, m) for m in (16, 8, 24)], axis=0)
+    (r,) = after([r], [xs[1], xs[3]])
+    own = [r] + [over_dp(r, 2 * a) for a in (1, 2, 3)]
+    other = [over_dp(p, 1) for p in own]
+    full_weight, rows = project(hidden_in, own, other, order, core, [decayed])
+    (rows,) = after([rows], [ts[1], ts[3]])
+    *hx, cut_done = split_hidden(x_place, hidden_in)
     bcs = [rows] + [over_seq(rows, k) for k in (1, 2, 3)]
+    near = after([hx[1], hx[3]], [own[3]])
+    hx1, hx3 = over_dp(near[0], 2), over_dp(near[1], 6)
+    hx = [hx[0], hx1, over_dp(hx[2], 4), hx3]
+    (bcs[0],) = after([bcs[0]], [hx1])
 
     outs = layer(place, xs, ts, bcs, grid, lead, write, weight, keep, skip)
     vgs, bgs = outs[:4], outs[4:]
@@ -364,22 +457,23 @@
     bc_grad = bc_grad.astype(BF)
     pieces = [vgs[0]] + [over_seq(vgs[k], k) for k in (1, 2, 3)]
 
-    send = dot_nn(turned[1].reshape(2048, BLOCK), bc_grad).astype(BF)
-    total = dot_nn(turned[0].reshape(2048, BLOCK), bc_grad)
-    total = (total + over_dp(send, 1).astype(F32)).reshape(4, 8, 64, 256)
-    came = [over_dp(total[a].astype(BF), 2 * a) for a in (1, 2, 3)]
-    total = total[0]
+    bc_grads = jnp.concatenate([bc_grad] + [over_dp(bc_grad, 2 * a) for a in (1, 2, 3)], axis=0)
+    turned = turn(pos, core, hx)
+    send = dot_nn(turned[1].reshape(512, 4 * BLOCK), bc_grads).astype(BF)
+    (send,) = after([send], [pieces[1], pieces[3]])
+    total = dot_nn(turned[0].reshape(512, 4 * BLOCK), bc_grads)
+    total = (total + over_dp(send, 1).astype(F32)).reshape(8, 64, 256)
+    half = total.astype(BF)
+    came = [over_dp(half[2:4], 16), over_dp(half[4:6], 8), over_dp(half[6:8], 24)]
+    total = total[0:2]
     for c in came:
         total = total + c.astype(F32)
-    for mask in (8, 16, 32):
-        half = total.shape[0] // 2
-        total = total[:half] + over_dp(total[half:].astype(BF), mask).astype(F32)
-    total = total[0]
-    for mask in (1, 2):
-        total = total + over_seq(total, mask)
+    (total,) = after([total], [pieces[2]])
+    total = total[0] + over_dp(total[1].astype(BF), 32).astype(F32)
 
     hidden_grad = dot_nt(bc_grad, full_weight).astype(BF)
     values_grad = gather_heads(place, pieces)
+    total = total + sum(over_seq(total, k) for k in (1, 2, 3))
     return values_grad, hidden_grad, total / math.sqrt(all_tokens)
 
 

time: 276 us -> 173 us (0.63); the launches traced: 271 us -> 171 us
  Pallas kernels: 121 us -> 43.6 us
  waiting for transfers between devices: 68.9 us -> 34.8 us
  starting transfers between devices: 51.2 us -> 56.9 us
  other arithmetic: 3.51 us -> 9.02 us
    pallas_call x1, Pallas kernels: 64.7 us -> 2.87 us  [gather_heads(): pl.pallas_call(gather_heads_kernel, in_specs=[smem()] + [anywhere()] * 4,...]
    ppermute x20 -> x18, waiting for transfers between devices: 35 us -> 6.19 us  [over_seq(): return lax.ppermute(x, 'seq', [(i, i ^ mask) for i in range(4)])]
    pallas_call x1 -> x11, Pallas kernels: 18.2 us -> 8.81 us  [the longest x1 3.76 us: cut_heads(): pl.pallas_call(cut_heads_kernel, in_specs=[smem()] + [anywhere()] * 3, ou...]
    ppermute x17 -> x22, starting transfers between devices: 24 us -> 32 us  [over_dp(): return lax.ppermute(x, 'dp', [(i, i ^ mask) for i in range(64)])]
    dynamic_slice x3 -> x1, local copies, waits for them, and re-layouts: 6.36 us -> 0.08 us  [body(): lax.dynamic_slice_in_dim(head_decay_rates, me * LOCAL_HEADS, LOCAL_HEADS)]
    ppermute x17 -> x22, waiting for transfers between devices: 33.8 us -> 28.6 us  [over_dp(): return lax.ppermute(x, 'dp', [(i, i ^ mask) for i in range(64)])]
    pallas_call x1, Pallas kernels: 24.8 us -> 21.2 us  [layer(): pl.pallas_call(layer_kernel, in_specs=[smem()] + [anywhere()] * 15 + [vme...]
    ppermute x20 -> x18, starting transfers between devices: 27.2 us -> 24.9 us  [over_seq(): return lax.ppermute(x, 'seq', [(i, i ^ mask) for i in range(4)])]
  transfers between devices with their start and end apart: 37 -> 40, of which waited for: 15 -> 12; matrix products, arithmetic and copies ran while one was open for 5% -> 12% of each run, Pallas kernels for 35% -> 25%
where the time goes in v2:
time: 173 us; the launch traced here: 171 us
  starting transfers between devices  56.9 us (33%)
  Pallas kernels  43.6 us (25%)
  waiting for transfers between devices  34.8 us (20%)
  local copies, waits for them, and re-layouts  20.3 us (12%)
  other arithmetic  9.02 us (5%)
  matrix products  5.58 us (3%)
    ppermute x22, starting transfers between devices, over_dp(): return lax.ppermute(x, 'dp', [(i, i ^ mask) for i in range(64)])  32 us
    ppermute x22, waiting for transfers between devices, over_dp(): return lax.ppermute(x, 'dp', [(i, i ^ mask) for i in range(64)])  28.6 us
    ppermute x18, starting transfers between devices, over_seq(): return lax.ppermute(x, 'seq', [(i, i ^ mask) for i in range(4)])  24.9 us
    pallas_call x1, Pallas kernels, layer(): pl.pallas_call(layer_kernel, in_specs=[smem()] + [anywhere()] * 15 + [vme...  21.2 us
    unnamed x73, local copies, waits for them, and re-layouts  12.1 us
    ppermute x18, waiting for transfers between devices, over_seq(): return lax.ppermute(x, 'seq', [(i, i ^ mask) for i in range(4)])  6.19 us
    pallas_call x1, Pallas kernels, decays(): pl.pallas_call(decay_kernel, grid=(PEERS,), in_specs=[blk(*small.shape[1:...  5.78 us
    pallas_call x1, Pallas kernels, project(): pl.pallas_call(project_kernel, in_specs=[smem(), smem(), vmem()] + [anywh...  4.95 us
  transfers between devices with their start and end apart: 40, of which 12 were waited for; matrix products, arithmetic and copies ran while one was open for 12% of the time, Pallas kernels for 25%

profile of v2, /device:TPU:2, one launch (start us, length us, event | category | flops | bytes accessed | tf_op | source)
XLA Modules:
  0.0 171.4 jit_solution(8392990317653249514)
XLA Ops:
  0.6 7.3 %collective-permute-start.6 = (bf16[1,64,256]{2,1,0:T(8,128)(2,1)}, bf16[1,64,256]{2,1,0:T(8,128)(2,1)S(1)}, u32[]{:S(2)}, u32[]{:S(2)}) collective-permute-start(bf16[1,64,256]{2,1,0:T(8,128)(2,1)} %bitcast.48), channel_id=1, source_target_pairs={{0,128},{4,132},{8,136},{12,140},{16,144},{20,148},{24,152},{28,15... | collective-permute-start | bytes 98312 | tf_op jit(solution)/shard_map/ppermute | solution.py:26
  12.4 3.8 %cut_heads.1 = (bf16[256,1152]{1,0:T(8,128)(2,1)}, bf16[256,1152]{1,0:T(8,128)(2,1)}, bf16[256,1152]{1,0:T(8,128)(2,1)}, bf16[256,1024]{1,0:T(8,128)(2,1)}, bf16...) custom-call(s32[1]{0:T(128)} %bitcast.place_ref, bf16[256,4096]{1,0:T(8,128)(2,1)} %refs_0_.1, ...), custom_call_target="tpu_custom_call" | custom-call | flops 1000 | bytes 6400000 | tf_op jit(solution)/shard_map/cut_heads/pallas_call | solution.py:132
  16.2 1.7 collective-permute-start
  17.9 2.2 %collective-permute-start.2 = (bf16[256,1152]{1,0:T(8,128)(2,1)}, bf16[256,1152]{1,0:T(8,128)(2,1)S(1)}, u32[]{:S(2)}, u32[]{:S(2)}) collective-permute-start(bf16[256,1152]{1,0:T(8,128)(2,1)} %get-tuple-element.33), channel_id=1, source_target_pairs={{0,3},{1,2},{2,1},{3,0},{4,7},{5,6},{6,5},{7,4},{8,11},{9,10},{10,... | collective-permute-start | bytes 1769480 | tf_op jit(solution)/shard_map/ppermute | solution.py:30
  21.0 3.2 %split_hidden.1 = (bf16[256,1024]{1,0:T(8,128)(2,1)}, bf16[256,1024]{1,0:T(8,128)(2,1)}, bf16[256,1024]{1,0:T(8,128)(2,1)}, bf16[256,1024]{1,0:T(8,128)(2,1)}, f32[8,128]{1,0:T(8,128)}) custom-call(s32[1]{0:T(128)} %bitcast.10.x_ref, bf16[256,4096]{1,0:T(8,128)(2,1)} %hidden_ref.3), custom_call_target="tpu_custom_call" | custom-call | flops 1000 | bytes 4200000 | tf_op jit(solution)/shard_map/split_hidden/pallas_call | solution.py:164
  25.1 2.0 %collective-permute-start.9 = (bf16[2,64,256]{2,1,0:T(8,128)(2,1)S(1)}, bf16[2,64,256]{2,1,0:T(8,128)(2,1)S(1)}, u32[]{:S(2)}, u32[]{:S(2)}) collective-permute-start(bf16[2,64,256]{2,1,0:T(8,128)(2,1)S(1)} %pad_maximum_fusion.4), channel_id=1, source_target_pairs={{0,96},{4,100},{8,104},{12,108},{16,112},{20,116},{24,120},{28,124... | collective-permute-start | bytes 196616 | tf_op jit(solution)/shard_map/ppermute | solution.py:26
  27.3 2.4 %collective-permute-start.7 = (bf16[2,64,256]{2,1,0:T(8,128)(2,1)S(1)}, bf16[2,64,256]{2,1,0:T(8,128)(2,1)S(1)}, u32[]{:S(2)}, u32[]{:S(2)}) collective-permute-start(bf16[2,64,256]{2,1,0:T(8,128)(2,1)S(1)} %pad_maximum_fusion.4), channel_id=1, source_target_pairs={{0,64},{4,68},{8,72},{12,76},{16,80},{20,84},{24,88},{28,92},{32,9... | collective-permute-start | bytes 196616 | tf_op jit(solution)/shard_map/ppermute | solution.py:26
  29.6 3.3 %collective-permute-done.7 = bf16[2,64,256]{2,1,0:T(8,128)(2,1)S(1)} collective-permute-done((bf16[2,64,256]{2,1,0:T(8,128)(2,1)S(1)}, bf16[2,64,256]{2,1,0:T(8,128)(2,1)S(1)}, u32[]{:S(2)}, u32[]{:S(2)}) %collective-permute-start.7) | collective-permute-done | bytes 65568 | tf_op jit(solution)/shard_map/ppermute | solution.py:26
  33.7 1.6 collective-permute-start.1
  36.9 1.5 collective-permute-start.12
  39.5 1.5 collective-permute-start.10
  42.7 8.8 %collective-permute-done.12.refs_3_.refs_2_ = bf16[8,64,256]{2,1,0:T(8,128)(2,1)S(1)} collective-permute-done((bf16[8,64,256]{2,1,0:T(8,128)(2,1)}, bf16[8,64,256]{2,1,0:T(8,128)(2,1)S(1)}, u32[]{:S(2)}, u32[]{:S(2)}) %collective-permute-start.12) | collective-permute-done | bytes 262176 | tf_op jit(solution)/shard_map/ppermute | solution.py:26
  52.2 1.8 %collective-permute-start.5 = (bf16[256,1024]{1,0:T(8,128)(2,1)}, bf16[256,1024]{1,0:T(8,128)(2,1)}, u32[]{:S(2)}, u32[]{:S(2)}) collective-permute-start(bf16[256,1024]{1,0:T(8,128)(2,1)} %get-tuple-element.38), channel_id=1, source_target_pairs={{0,3},{1,2},{2,1},{3,0},{4,7},{5,6},{6,5},{7,4},{8,11},{9,10},{10,... | collective-permute-start | bytes 1572872 | tf_op jit(solution)/shard_map/ppermute | solution.py:30
  57.0 1.9 %collective-permute-start.4 = (bf16[256,1024]{1,0:T(8,128)(2,1)}, bf16[256,1024]{1,0:T(8,128)(2,1)}, u32[]{:S(2)}, u32[]{:S(2)}) collective-permute-start(bf16[256,1024]{1,0:T(8,128)(2,1)} %get-tuple-element.37), channel_id=1, source_target_pairs={{0,2},{1,3},{2,0},{3,1},{4,6},{5,7},{6,4},{7,5},{8,10},{9,11},{10,... | collective-permute-start | bytes 1572872 | tf_op jit(solution)/shard_map/ppermute | solution.py:30
  58.9 1.8 %collective-permute-start.17 = (bf16[256,1024]{1,0:T(8,128)(2,1)}, bf16[256,1024]{1,0:T(8,128)(2,1)S(1)}, u32[]{:S(2)}, u32[]{:S(2)}) collective-permute-start(bf16[256,1024]{1,0:T(8,128)(2,1)} %get-tuple-element.43), channel_id=1, source_target_pairs={{0,8},{4,12},{8,0},{12,4},{16,24},{20,28},{24,16},{28,20},{32,40},... | collective-permute-start | bytes 1572872 | tf_op jit(solution)/shard_map/ppermute | solution.py:26
  60.8 5.8 %decays.1 = (bf16[4,16,256,256]{3,2,1,0:T(8,128)(2,1)S(1)}, bf16[4,256,1024]{2,1,0:T(8,128)(2,1)S(1)}, bf16[4,256,1024]{2,1,0:T(8,128)(2,1)S(1)}, f32[8,128]{1,0:T(8,128)S(1)}) custom-call(f32[4,32,256]{2,1,0:T(8,128)S(1)} %pad_maximum_fusion.1.small_ref), custom_call_target="tpu_custom_call" | custom-call | flops 40000000 | bytes 17000000 | tf_op jit(solution)/shard_map/decays/pallas_call | solution.py:94
  66.6 3.3 %copy-done = bf16[4,16,256,256]{3,2,1,0:T(8,128)(2,1)} copy-done((bf16[4,16,256,256]{3,2,1,0:T(8,128)(2,1)}, bf16[4,16,256,256]{3,2,1,0:T(8,128)(2,1)S(1)}, u32[]{:S(2)}) %copy-start) | copy-done | bytes 8388632
  70.0 1.1 copy-done.13
  71.1 1.2 copy-done.15
  73.2 5.0 %project.1 = (bf16[4096,256]{1,0:T(8,128)(2,1)S(1)}, bf16[256,256]{1,0:T(8,128)(2,1)S(1)}) custom-call(s32[32]{0:T(128)S(1)} %broadcast_xor_fusion.order_ref, s32[1]{0:T(128)} %bitcast.2.core_ref, bf16[256,4096]{1,0:T(8,128)(2,1)S(1)} %copy-done.1, bf16[8,64,256]{2,1,0:T(8,128)(2,1)S(1)} %copy-done.7, bf16[8,64,256]{2,1,0:T(8,128)(2,1)S(1)} %copy-done.13, ...), custom_call_target="tpu_custom_call" | custom-call | flops 540000000 | bytes 6000000 | tf_op jit(solution)/shard_map/project/pallas_call | solution.py:218
  78.9 1.7 collective-permute-start.20
  81.6 1.3 collective-permute-start.18
  83.9 2.7 %multiply_divide_fusion.refs_15_ = f32[4,256,1]{2,1,0:T(8,128)} fusion(f32[4,256,128]{2,1,0:T(8,128)} %copy-done.19, f32[]{:T(128)} %get-tuple-element.59), kind=kLoop, calls=%fused_computation.11 | loop fusion | flops 2048 | bytes 8196 | tf_op jit(solution)/shard_map/div | solution.py:431
  86.6 1.4 collective-permute-done.20.refs_11_
  88.0 1.5 collective-permute-start.27
  89.6 1.3 collective-permute-start.28
  91.8 21.2 %layer.1 = (bf16[256,1024]{1,0:T(8,128)(2,1)}, bf16[256,1024]{1,0:T(8,128)(2,1)}, bf16[256,1024]{1,0:T(8,128)(2,1)}, bf16[256,1024]{1,0:T(8,128)(2,1)}, f32[256,...) custom-call(s32[1]{0:T(128)} %bitcast.place_ref, ...), custom_call_target="tpu_custom_call" | custom-call | flops 5000000000 | bytes 24000000 | tf_op jit(solution)/shard_map/layer/pallas_call | solution.py:316
  113.2 2.8 %collective-permute-start.25 = (bf16[256,256]{1,0:T(8,128)(2,1)}, bf16[256,256]{1,0:T(8,128)(2,1)S(1)}, u32[]{:S(2)}, u32[]{:S(2)}) collective-permute-start(bf16[256,256]{1,0:T(8,128)(2,1)} %get-tuple-element.53), channel_id=1, source_target_pairs={{0,2},{1,3},{2,0},{3,1},{4,6},{5,7},{6,4},{7,5},{8,10},{9,11},{10,... | collective-permute-start | bytes 393224 | tf_op jit(solution)/shard_map/ppermute | solution.py:30
  116.0 1.7 %collective-permute-start.26 = (bf16[256,256]{1,0:T(8,128)(2,1)}, bf16[256,256]{1,0:T(8,128)(2,1)S(1)}, u32[]{:S(2)}, u32[]{:S(2)}) collective-permute-start(bf16[256,256]{1,0:T(8,128)(2,1)} %get-tuple-element.54), channel_id=1, source_target_pairs={{0,3},{1,2},{2,1},{3,0},{4,7},{5,6},{6,5},{7,4},{8,11},{9,10},{10,... | collective-permute-start | bytes 393224 | tf_op jit(solution)/shard_map/ppermute | solution.py:30
  118.6 1.6 collective-permute-start.23
  120.1 1.8 %turn.1 = bf16[2,8,64,1024]{3,2,1,0:T(8,128)(2,1)S(1)} custom-call(s32[8]{0:T(128)S(1)} %gather_fusion, s32[1]{0:T(128)} %bitcast.2.core_ref, bf16[256,1024]{1,0:T(8,128)(2,1)S(1)} %copy-done.11, bf16[256,1024]{1,0:T(8,128)(2,1)S(1)} %copy-done.5, bf16[256,1024]{1,0:T(8,128)(2,1)} %collective-permute-done.27.p2, bf16[256,1024]{1,0:T(8,128)(2,1)} %collective-permute-done.28.p3), custom_call_target="tpu_custom_call" | custom-call | flops 1000 | bytes 14000000 | tf_op jit(solution)/shard_map/turn/pallas_call | solution.py:186
  122.3 2.2 %collective-permute-done.26 = bf16[256,256]{1,0:T(8,128)(2,1)S(1)} collective-permute-done((bf16[256,256]{1,0:T(8,128)(2,1)}, bf16[256,256]{1,0:T(8,128)(2,1)S(1)}, u32[]{:S(2)}, u32[]{:S(2)}) %collective-permute-start.26) | collective-permute-done | bytes 131104 | tf_op jit(solution)/shard_map/ppermute | solution.py:30
  125.2 3.9 %collective-permute-start.30 = (bf16[256,256]{1,0:T(8,128)(2,1)S(1)}, bf16[256,256]{1,0:T(8,128)(2,1)S(1)}, u32[]{:S(2)}, u32[]{:S(2)}) collective-permute-start(bf16[256,256]{1,0:T(8,128)(2,1)S(1)} %add_convert_fusion), channel_id=1, source_target_pairs={{0,16},{4,20},{8,24},{12,28},{16,0},{20,4},{24,8},{28,12},{32,48},... | collective-permute-start | bytes 393224 | tf_op jit(solution)/shard_map/ppermute | solution.py:26
  132.0 2.1 %collective-permute-done.29 = bf16[256,256]{1,0:T(8,128)(2,1)S(1)} collective-permute-done((bf16[256,256]{1,0:T(8,128)(2,1)S(1)}, bf16[256,256]{1,0:T(8,128)(2,1)S(1)}, u32[]{:S(2)}, u32[]{:S(2)}) %collective-permute-start.29) | collective-permute-done | bytes 131104 | tf_op jit(solution)/shard_map/ppermute | solution.py:26
  134.1 1.1 convolution_convert_fusion.1.refs_0_
  135.7 1.4 collective-permute-done.32
  137.1 1.7 fusion.24
  138.8 2.0 %collective-permute-start.35 = (bf16[2,64,256]{2,1,0:T(8,128)(2,1)S(1)}, bf16[2,64,256]{2,1,0:T(8,128)(2,1)S(1)}, u32[]{:S(2)}, u32[]{:S(2)}) collective-permute-start(bf16[2,64,256]{2,1,0:T(8,128)(2,1)S(1)} %bitcast.52), channel_id=1, source_target_pairs={{0,96},{4,100},{8,104},{12,108},{16,112},{20,116},{24,120},{28,124... | collective-permute-start | bytes 196616 | tf_op jit(solution)/shard_map/ppermute | solution.py:26
  140.8 1.2 collective-permute-start.33
  141.9 1.4 collective-permute-start.34
  143.3 2.3 %collective-permute-done.35 = bf16[2,64,256]{2,1,0:T(8,128)(2,1)S(1)} collective-permute-done((bf16[2,64,256]{2,1,0:T(8,128)(2,1)S(1)}, bf16[2,64,256]{2,1,0:T(8,128)(2,1)S(1)}, u32[]{:S(2)}, u32[]{:S(2)}) %collective-permute-start.35) | collective-permute-done | bytes 65568 | tf_op jit(solution)/shard_map/ppermute | solution.py:26
  145.6 2.7 %collective-permute-done.33 = bf16[2,64,256]{2,1,0:T(8,128)(2,1)S(1)} collective-permute-done((bf16[2,64,256]{2,1,0:T(8,128)(2,1)S(1)}, bf16[2,64,256]{2,1,0:T(8,128)(2,1)S(1)}, u32[]{:S(2)}, u32[]{:S(2)}) %collective-permute-start.33) | collective-permute-done | bytes 65568 | tf_op jit(solution)/shard_map/ppermute | solution.py:26
  149.0 2.2 %collective-permute-done.22.p2.refs_1_ = bf16[256,1024]{1,0:T(8,128)(2,1)S(1)} collective-permute-done((bf16[256,1024]{1,0:T(8,128)(2,1)S(1)}, bf16[256,1024]{1,0:T(8,128)(2,1)S(1)}, u32[]{:S(2)}, u32[]{:S(2)}) %collective-permute-start.22) | collective-permute-done | bytes 524320 | tf_op jit(solution)/shard_map/ppermute | solution.py:30
  153.9 6.9 %collective-permute-done.36 = bf16[64,256]{1,0:T(8,128)(2,1)S(1)} collective-permute-done((bf16[64,256]{1,0:T(8,128)(2,1)S(1)}, bf16[64,256]{1,0:T(8,128)(2,1)S(1)}, u32[]{:S(2)}, u32[]{:S(2)}) %collective-permute-start.36) | collective-permute-done | bytes 32800 | tf_op jit(solution)/shard_map/ppermute | solution.py:26
  161.7 1.4 collective-permute-start.39
  163.0 2.7 %collective-permute-start.37 = (f32[64,256]{1,0:T(8,128)S(1)}, f32[64,256]{1,0:T(8,128)S(1)}, u32[]{:S(2)}, u32[]{:S(2)}) collective-permute-start(f32[64,256]{1,0:T(8,128)S(1)} %fusion.14), channel_id=1, source_target_pairs={{0,1},{1,0},{2,3},{3,2},{4,5},{5,4},{6,7},{7,6},{8,9},{9,8},{10,11... | collective-permute-start | bytes 196616 | tf_op jit(solution)/shard_map/ppermute | solution.py:30
  165.8 2.1 %convolution_convert_fusion = bf16[256,4096]{1,0:T(8,128)(2,1)} fusion(bf16[256,256]{1,0:T(8,128)(2,1)S(1)} %add_convert_fusion, bf16[4096,256]{1,0:T(8,128)(2,1)S(1)} %get-tuple-element.55), kind=kOutput, calls=%fused_computation.1 | convolution fusion | flops 537919488 | bytes 4325376 | tf_op jit(solution)/shard_map/dot_general | solution.py:38
  167.8 2.9 %gather_heads.1 = bf16[256,4096]{1,0:T(8,128)(2,1)} custom-call(s32[1]{0:T(128)} %bitcast.place_ref, bf16[256,1024]{1,0:T(8,128)(2,1)} %get-tuple-element.47.p0, bf16[256,1024]{1,0:T(8,128)(2,1)} %collective-permute-done.21.p1.refs_1_, bf16[256,1024]{1,0:T(8,128)(2,1)} %copy-done.22, bf16[256,1024]{1,0:T(8,128)(2,1)} %collective-permute-done.23.p3.refs_2_), custom_call_target="tpu_custom_call" | custom-call | flops 1000 | bytes 4200000 | tf_op jit(solution)/shard_map/gather_heads/pallas_call | solution.py:360
  (164 shorter events, 30.0 us)
Async XLA Ops:
  0.6 24.5 %collective-permute-start.6 = (bf16[1,64,256]{2,1,0:T(8,128)(2,1)}, bf16[1,64,256]{2,1,0:T(8,128)(2,1)S(1)}, u32[]{:S(2)}, u32[]{:S(2)}) collective-permute-start(bf16[1,64,256]{2,1,0:T(8,128)(2,1)} %bitcast.48), channel_id=1, source_target_pairs={{0,128},{4,132},{8,136},{12,140},{16,144},{20,148},{24,152},{28,15... | collective-permute-start | bytes 98312 | tf_op jit(solution)/shard_map/ppermute | solution.py:26
  16.2 16.6 %collective-permute-start = (bf16[256,1152]{1,0:T(8,128)(2,1)}, bf16[256,1152]{1,0:T(8,128)(2,1)S(1)}, u32[]{:S(2)}, u32[]{:S(2)}) collective-permute-start(bf16[256,1152]{1,0:T(8,128)(2,1)} %get-tuple-element.31), channel_id=1, source_target_pairs={{0,1},{1,0},{2,3},{3,2},{4,5},{5,4},{6,7},{7,6},{8,9},{9,8},{10,11... | collective-permute-start | bytes 1769480 | tf_op jit(solution)/shard_map/ppermute | solution.py:30
  17.9 17.5 %collective-permute-start.2 = (bf16[256,1152]{1,0:T(8,128)(2,1)}, bf16[256,1152]{1,0:T(8,128)(2,1)S(1)}, u32[]{:S(2)}, u32[]{:S(2)}) collective-permute-start(bf16[256,1152]{1,0:T(8,128)(2,1)} %get-tuple-element.33), channel_id=1, source_target_pairs={{0,3},{1,2},{2,1},{3,0},{4,7},{5,6},{6,5},{7,4},{8,11},{9,10},{10,... | collective-permute-start | bytes 1769480 | tf_op jit(solution)/shard_map/ppermute | solution.py:30
  25.1 10.2 %collective-permute-start.9 = (bf16[2,64,256]{2,1,0:T(8,128)(2,1)S(1)}, bf16[2,64,256]{2,1,0:T(8,128)(2,1)S(1)}, u32[]{:S(2)}, u32[]{:S(2)}) collective-permute-start(bf16[2,64,256]{2,1,0:T(8,128)(2,1)S(1)} %pad_maximum_fusion.4), channel_id=1, source_target_pairs={{0,96},{4,100},{8,104},{12,108},{16,112},{20,116},{24,120},{28,124... | collective-permute-start | bytes 196616 | tf_op jit(solution)/shard_map/ppermute | solution.py:26
  27.1 8.2 %collective-permute-start.8 = (bf16[2,64,256]{2,1,0:T(8,128)(2,1)S(1)}, bf16[2,64,256]{2,1,0:T(8,128)(2,1)S(1)}, u32[]{:S(2)}, u32[]{:S(2)}) collective-permute-start(bf16[2,64,256]{2,1,0:T(8,128)(2,1)S(1)} %pad_maximum_fusion.4), channel_id=1, source_target_pairs={{0,32},{4,36},{8,40},{12,44},{16,48},{20,52},{24,56},{28,60},{32,0... | collective-permute-start | bytes 196616 | tf_op jit(solution)/shard_map/ppermute | solution.py:26
  27.3 5.6 %collective-permute-start.7 = (bf16[2,64,256]{2,1,0:T(8,128)(2,1)S(1)}, bf16[2,64,256]{2,1,0:T(8,128)(2,1)S(1)}, u32[]{:S(2)}, u32[]{:S(2)}) collective-permute-start(bf16[2,64,256]{2,1,0:T(8,128)(2,1)S(1)} %pad_maximum_fusion.4), channel_id=1, source_target_pairs={{0,64},{4,68},{8,72},{12,76},{16,80},{20,84},{24,88},{28,92},{32,9... | collective-permute-start | bytes 196616 | tf_op jit(solution)/shard_map/ppermute | solution.py:26
  33.7 18.5 %collective-permute-start.1 = (bf16[256,1152]{1,0:T(8,128)(2,1)}, bf16[256,1152]{1,0:T(8,128)(2,1)S(1)}, u32[]{:S(2)}, u32[]{:S(2)}) collective-permute-start(bf16[256,1152]{1,0:T(8,128)(2,1)} %after.8), channel_id=1, source_target_pairs={{0,2},{1,3},{2,0},{3,1},{4,6},{5,7},{6,4},{7,5},{8,10},{9,11},{10,... | collective-permute-start | bytes 1769480 | tf_op jit(solution)/shard_map/ppermute | solution.py:30
  36.9 17.3 %collective-permute-start.13 = (bf16[8,64,256]{2,1,0:T(8,128)(2,1)}, bf16[8,64,256]{2,1,0:T(8,128)(2,1)S(1)}, u32[]{:S(2)}, u32[]{:S(2)}) collective-permute-start(bf16[8,64,256]{2,1,0:T(8,128)(2,1)} %after.10.refs_0_), channel_id=1, source_target_pairs={{0,4},{4,0},{8,12},{12,8},{16,20},{20,16},{24,28},{28,24},{32,36},... | collective-permute-start | bytes 786440 | tf_op jit(solution)/shard_map/ppermute | solution.py:26
  36.9 14.5 %collective-permute-start.12 = (bf16[8,64,256]{2,1,0:T(8,128)(2,1)}, bf16[8,64,256]{2,1,0:T(8,128)(2,1)S(1)}, u32[]{:S(2)}, u32[]{:S(2)}) collective-permute-start(bf16[8,64,256]{2,1,0:T(8,128)(2,1)} %after.10.refs_0_), channel_id=1, source_target_pairs={{0,24},{4,28},{8,16},{12,20},{16,8},{20,12},{24,0},{28,4},{32,56},... | collective-permute-start | bytes 786440 | tf_op jit(solution)/shard_map/ppermute | solution.py:26
  38.4 15.9 %collective-permute-start.11 = (bf16[8,64,256]{2,1,0:T(8,128)(2,1)}, bf16[8,64,256]{2,1,0:T(8,128)(2,1)S(1)}, u32[]{:S(2)}, u32[]{:S(2)}) collective-permute-start(bf16[8,64,256]{2,1,0:T(8,128)(2,1)} %after.10.refs_0_), channel_id=1, source_target_pairs={{0,16},{4,20},{8,24},{12,28},{16,0},{20,4},{24,8},{28,12},{32,48},... | collective-permute-start | bytes 786440 | tf_op jit(solution)/shard_map/ppermute | solution.py:26
  39.5 16.5 %collective-permute-start.10 = (bf16[8,64,256]{2,1,0:T(8,128)(2,1)}, bf16[8,64,256]{2,1,0:T(8,128)(2,1)S(1)}, u32[]{:S(2)}, u32[]{:S(2)}) collective-permute-start(bf16[8,64,256]{2,1,0:T(8,128)(2,1)} %after.10.refs_0_), channel_id=1, source_target_pairs={{0,8},{4,12},{8,0},{12,4},{16,24},{20,28},{24,16},{28,20},{32,40},... | collective-permute-start | bytes 786440 | tf_op jit(solution)/shard_map/ppermute | solution.py:26
  51.5 27.4 %collective-permute-start.3 = (bf16[256,1024]{1,0:T(8,128)(2,1)}, bf16[256,1024]{1,0:T(8,128)(2,1)}, u32[]{:S(2)}, u32[]{:S(2)}) collective-permute-start(bf16[256,1024]{1,0:T(8,128)(2,1)} %get-tuple-element.36), channel_id=1, source_target_pairs={{0,1},{1,0},{2,3},{3,2},{4,5},{5,4},{6,7},{7,6},{8,9},{9,8},{10,11... | collective-permute-start | bytes 1572872 | tf_op jit(solution)/shard_map/ppermute | solution.py:30
  52.2 26.7 %collective-permute-start.5 = (bf16[256,1024]{1,0:T(8,128)(2,1)}, bf16[256,1024]{1,0:T(8,128)(2,1)}, u32[]{:S(2)}, u32[]{:S(2)}) collective-permute-start(bf16[256,1024]{1,0:T(8,128)(2,1)} %get-tuple-element.38), channel_id=1, source_target_pairs={{0,3},{1,2},{2,1},{3,0},{4,7},{5,6},{6,5},{7,4},{8,11},{9,10},{10,... | collective-permute-start | bytes 1572872 | tf_op jit(solution)/shard_map/ppermute | solution.py:30
  54.2 2.7 %collective-permute-start.16 = (bf16[8,64,256]{2,1,0:T(8,128)(2,1)}, bf16[8,64,256]{2,1,0:T(8,128)(2,1)S(1)}, u32[]{:S(2)}, u32[]{:S(2)}) collective-permute-start(bf16[8,64,256]{2,1,0:T(8,128)(2,1)} %copy-done.9), channel_id=1, source_target_pairs={{0,4},{4,0},{8,12},{12,8},{16,20},{20,16},{24,28},{28,24},{32,36},... | collective-permute-start | bytes 786440 | tf_op jit(solution)/shard_map/ppermute | solution.py:26
  54.3 4.6 %collective-permute-start.15 = (bf16[8,64,256]{2,1,0:T(8,128)(2,1)S(1)}, bf16[8,64,256]{2,1,0:T(8,128)(2,1)S(1)}, u32[]{:S(2)}, u32[]{:S(2)}) collective-permute-start(bf16[8,64,256]{2,1,0:T(8,128)(2,1)S(1)} %collective-permute-done.11.refs_2_), channel_id=1, source_target_pairs={{0,4},{4,0},{8,12},{12,8},{16,20},{20,16},{24,28},{28,24},{32,36},... | collective-permute-start | bytes 786440 | tf_op jit(solution)/shard_map/ppermute | solution.py:26
  56.1 10.5 %copy-start.12 = (bf16[8,64,256]{2,1,0:T(8,128)(2,1)}, bf16[8,64,256]{2,1,0:T(8,128)(2,1)S(1)}, u32[]{:S(2)}) copy-start(bf16[8,64,256]{2,1,0:T(8,128)(2,1)S(1)} %collective-permute-done.10.refs_1_) | copy-start | bytes 786436
  56.1 13.9 %collective-permute-start.14 = (bf16[8,64,256]{2,1,0:T(8,128)(2,1)S(1)}, bf16[8,64,256]{2,1,0:T(8,128)(2,1)S(1)}, u32[]{:S(2)}, u32[]{:S(2)}) collective-permute-start(bf16[8,64,256]{2,1,0:T(8,128)(2,1)S(1)} %collective-permute-done.10.refs_1_), channel_id=1, source_target_pairs={{0,4},{4,0},{8,12},{12,8},{16,20},{20,16},{24,28},{28,24},{32,36},... | collective-permute-start | bytes 786440 | tf_op jit(solution)/shard_map/ppermute | solution.py:26
  57.0 9.6 %copy-start.14 = (bf16[8,64,256]{2,1,0:T(8,128)(2,1)}, bf16[8,64,256]{2,1,0:T(8,128)(2,1)S(1)}, u32[]{:S(2)}) copy-start(bf16[8,64,256]{2,1,0:T(8,128)(2,1)S(1)} %collective-permute-done.16.refs_7_) | copy-start | bytes 786436
  57.0 34.7 %collective-permute-start.4 = (bf16[256,1024]{1,0:T(8,128)(2,1)}, bf16[256,1024]{1,0:T(8,128)(2,1)}, u32[]{:S(2)}, u32[]{:S(2)}) collective-permute-start(bf16[256,1024]{1,0:T(8,128)(2,1)} %get-tuple-element.37), channel_id=1, source_target_pairs={{0,2},{1,3},{2,0},{3,1},{4,6},{5,7},{6,4},{7,5},{8,10},{9,11},{10,... | collective-permute-start | bytes 1572872 | tf_op jit(solution)/shard_map/ppermute | solution.py:30
  58.9 32.0 %collective-permute-start.17 = (bf16[256,1024]{1,0:T(8,128)(2,1)}, bf16[256,1024]{1,0:T(8,128)(2,1)S(1)}, u32[]{:S(2)}, u32[]{:S(2)}) collective-permute-start(bf16[256,1024]{1,0:T(8,128)(2,1)} %get-tuple-element.43), channel_id=1, source_target_pairs={{0,8},{4,12},{8,0},{12,4},{16,24},{20,28},{24,16},{28,20},{32,40},... | collective-permute-start | bytes 1572872 | tf_op jit(solution)/shard_map/ppermute | solution.py:26
  60.7 9.2 %copy-start.1 = (bf16[256,4096]{1,0:T(8,128)(2,1)S(1)}, bf16[256,4096]{1,0:T(8,128)(2,1)}, u32[]{:S(2)}) copy-start(bf16[256,4096]{1,0:T(8,128)(2,1)} %hidden_ref.3) | copy-start | bytes 6291460
  60.8 9.2 %copy-start.7 = (bf16[8,64,256]{2,1,0:T(8,128)(2,1)S(1)}, bf16[8,64,256]{2,1,0:T(8,128)(2,1)}, u32[]{:S(2)}) copy-start(bf16[8,64,256]{2,1,0:T(8,128)(2,1)} %after.10.refs_0_) | copy-start | bytes 786436
  60.8 9.2 %copy-start.10 = (bf16[8,64,256]{2,1,0:T(8,128)(2,1)S(1)}, bf16[8,64,256]{2,1,0:T(8,128)(2,1)}, u32[]{:S(2)}) copy-start(bf16[8,64,256]{2,1,0:T(8,128)(2,1)} %copy-done.9) | copy-start | bytes 786436
  78.9 9.2 %collective-permute-start.20 = (bf16[256,256]{1,0:T(8,128)(2,1)}, bf16[256,256]{1,0:T(8,128)(2,1)S(1)}, u32[]{:S(2)}, u32[]{:S(2)}) collective-permute-start(bf16[256,256]{1,0:T(8,128)(2,1)} %after.11.refs_0_), channel_id=1, source_target_pairs={{0,3},{1,2},{2,1},{3,0},{4,7},{5,6},{6,5},{7,4},{8,11},{9,10},{10,... | collective-permute-start | bytes 393224 | tf_op jit(solution)/shard_map/ppermute | solution.py:30
  80.6 9.0 %collective-permute-start.19 = (bf16[256,256]{1,0:T(8,128)(2,1)}, bf16[256,256]{1,0:T(8,128)(2,1)S(1)}, u32[]{:S(2)}, u32[]{:S(2)}) collective-permute-start(bf16[256,256]{1,0:T(8,128)(2,1)} %after.11.refs_0_), channel_id=1, source_target_pairs={{0,2},{1,3},{2,0},{3,1},{4,6},{5,7},{6,4},{7,5},{8,10},{9,11},{10,... | collective-permute-start | bytes 393224 | tf_op jit(solution)/shard_map/ppermute | solution.py:30
  81.6 9.3 %collective-permute-start.18 = (bf16[256,256]{1,0:T(8,128)(2,1)}, bf16[256,256]{1,0:T(8,128)(2,1)S(1)}, u32[]{:S(2)}, u32[]{:S(2)}) collective-permute-start(bf16[256,256]{1,0:T(8,128)(2,1)} %after.11.refs_0_), channel_id=1, source_target_pairs={{0,1},{1,0},{2,3},{3,2},{4,5},{5,4},{6,7},{7,6},{8,9},{9,8},{10,11... | collective-permute-start | bytes 393224 | tf_op jit(solution)/shard_map/ppermute | solution.py:30
  88.0 30.4 %collective-permute-start.27 = (bf16[256,1024]{1,0:T(8,128)(2,1)}, bf16[256,1024]{1,0:T(8,128)(2,1)}, u32[]{:S(2)}, u32[]{:S(2)}) collective-permute-start(bf16[256,1024]{1,0:T(8,128)(2,1)} %get-tuple-element.57), channel_id=1, source_target_pairs={{0,16},{4,20},{8,24},{12,28},{16,0},{20,4},{24,8},{28,12},{32,48},... | collective-permute-start | bytes 1572872 | tf_op jit(solution)/shard_map/ppermute | solution.py:26
  89.6 29.0 %collective-permute-start.28 = (bf16[256,1024]{1,0:T(8,128)(2,1)}, bf16[256,1024]{1,0:T(8,128)(2,1)}, u32[]{:S(2)}, u32[]{:S(2)}) collective-permute-start(bf16[256,1024]{1,0:T(8,128)(2,1)} %get-tuple-element.58), channel_id=1, source_target_pairs={{0,24},{4,28},{8,16},{12,20},{16,8},{20,12},{24,0},{28,4},{32,56},... | collective-permute-start | bytes 1572872 | tf_op jit(solution)/shard_map/ppermute | solution.py:26
  91.7 26.0 %copy-start.18 = (s32[8]{0:T(128)S(1)}, s32[8]{0:T(128)}, u32[]{:S(2)}) copy-start(s32[8]{0:T(128)} %constant.90.clone) | copy-start | bytes 100
  91.8 28.4 %copy-start.5 = (bf16[256,1024]{1,0:T(8,128)(2,1)S(1)}, bf16[256,1024]{1,0:T(8,128)(2,1)}, u32[]{:S(2)}) copy-start(bf16[256,1024]{1,0:T(8,128)(2,1)} %copy-done.4) | copy-start | bytes 1572868
  91.8 28.4 %copy-start.11 = (bf16[256,1024]{1,0:T(8,128)(2,1)S(1)}, bf16[256,1024]{1,0:T(8,128)(2,1)}, u32[]{:S(2)}) copy-start(bf16[256,1024]{1,0:T(8,128)(2,1)} %get-tuple-element.56.p0) | copy-start | bytes 1572868
  113.0 9.0 %collective-permute-start.24 = (bf16[256,256]{1,0:T(8,128)(2,1)}, bf16[256,256]{1,0:T(8,128)(2,1)S(1)}, u32[]{:S(2)}, u32[]{:S(2)}) collective-permute-start(bf16[256,256]{1,0:T(8,128)(2,1)} %get-tuple-element.52), channel_id=1, source_target_pairs={{0,1},{1,0},{2,3},{3,2},{4,5},{5,4},{6,7},{7,6},{8,9},{9,8},{10,11... | collective-permute-start | bytes 393224 | tf_op jit(solution)/shard_map/ppermute | solution.py:30
  113.2 9.1 %collective-permute-start.25 = (bf16[256,256]{1,0:T(8,128)(2,1)}, bf16[256,256]{1,0:T(8,128)(2,1)S(1)}, u32[]{:S(2)}, u32[]{:S(2)}) collective-permute-start(bf16[256,256]{1,0:T(8,128)(2,1)} %get-tuple-element.53), channel_id=1, source_target_pairs={{0,2},{1,3},{2,0},{3,1},{4,6},{5,7},{6,4},{7,5},{8,10},{9,11},{10,... | collective-permute-start | bytes 393224 | tf_op jit(solution)/shard_map/ppermute | solution.py:30
  116.0 8.5 %collective-permute-start.26 = (bf16[256,256]{1,0:T(8,128)(2,1)}, bf16[256,256]{1,0:T(8,128)(2,1)S(1)}, u32[]{:S(2)}, u32[]{:S(2)}) collective-permute-start(bf16[256,256]{1,0:T(8,128)(2,1)} %get-tuple-element.54), channel_id=1, source_target_pairs={{0,3},{1,2},{2,1},{3,0},{4,7},{5,6},{6,5},{7,4},{8,11},{9,10},{10,... | collective-permute-start | bytes 393224 | tf_op jit(solution)/shard_map/ppermute | solution.py:30
  118.4 16.8 %collective-permute-start.21 = (bf16[256,1024]{1,0:T(8,128)(2,1)}, bf16[256,1024]{1,0:T(8,128)(2,1)}, u32[]{:S(2)}, u32[]{:S(2)}) collective-permute-start(bf16[256,1024]{1,0:T(8,128)(2,1)} %get-tuple-element.48), channel_id=1, source_target_pairs={{0,1},{1,0},{2,3},{3,2},{4,5},{5,4},{6,7},{7,6},{8,9},{9,8},{10,11... | collective-permute-start | bytes 1572872 | tf_op jit(solution)/shard_map/ppermute | solution.py:30
  118.6 16.7 %collective-permute-start.23 = (bf16[256,1024]{1,0:T(8,128)(2,1)}, bf16[256,1024]{1,0:T(8,128)(2,1)}, u32[]{:S(2)}, u32[]{:S(2)}) collective-permute-start(bf16[256,1024]{1,0:T(8,128)(2,1)} %get-tuple-element.50), channel_id=1, source_target_pairs={{0,3},{1,2},{2,1},{3,0},{4,7},{5,6},{6,5},{7,4},{8,11},{9,10},{10,... | collective-permute-start | bytes 1572872 | tf_op jit(solution)/shard_map/ppermute | solution.py:30
  124.6 6.3 %collective-permute-start.31 = (bf16[256,256]{1,0:T(8,128)(2,1)S(1)}, bf16[256,256]{1,0:T(8,128)(2,1)S(1)}, u32[]{:S(2)}, u32[]{:S(2)}) collective-permute-start(bf16[256,256]{1,0:T(8,128)(2,1)S(1)} %add_convert_fusion), channel_id=1, source_target_pairs={{0,24},{4,28},{8,16},{12,20},{16,8},{20,12},{24,0},{28,4},{32,56},... | collective-permute-start | bytes 393224 | tf_op jit(solution)/shard_map/ppermute | solution.py:26
  125.2 6.8 %collective-permute-start.30 = (bf16[256,256]{1,0:T(8,128)(2,1)S(1)}, bf16[256,256]{1,0:T(8,128)(2,1)S(1)}, u32[]{:S(2)}, u32[]{:S(2)}) collective-permute-start(bf16[256,256]{1,0:T(8,128)(2,1)S(1)} %add_convert_fusion), channel_id=1, source_target_pairs={{0,16},{4,20},{8,24},{12,28},{16,0},{20,4},{24,8},{28,12},{32,48},... | collective-permute-start | bytes 393224 | tf_op jit(solution)/shard_map/ppermute | solution.py:26
  129.1 5.0 %collective-permute-start.29 = (bf16[256,256]{1,0:T(8,128)(2,1)S(1)}, bf16[256,256]{1,0:T(8,128)(2,1)S(1)}, u32[]{:S(2)}, u32[]{:S(2)}) collective-permute-start(bf16[256,256]{1,0:T(8,128)(2,1)S(1)} %add_convert_fusion), channel_id=1, source_target_pairs={{0,8},{4,12},{8,0},{12,4},{16,24},{20,28},{24,16},{28,20},{32,40},... | collective-permute-start | bytes 393224 | tf_op jit(solution)/shard_map/ppermute | solution.py:26
  135.3 1.8 %collective-permute-start.32 = (bf16[512,256]{1,0:T(8,128)(2,1)}, bf16[512,256]{1,0:T(8,128)(2,1)S(1)}, u32[]{:S(2)}, u32[]{:S(2)}) collective-permute-start(bf16[512,256]{1,0:T(8,128)(2,1)} %after.14), channel_id=1, source_target_pairs={{0,4},{4,0},{8,12},{12,8},{16,20},{20,16},{24,28},{28,24},{32,36},... | collective-permute-start | bytes 786440 | tf_op jit(solution)/shard_map/ppermute | solution.py:26
  135.4 15.8 %collective-permute-start.22 = (bf16[256,1024]{1,0:T(8,128)(2,1)S(1)}, bf16[256,1024]{1,0:T(8,128)(2,1)S(1)}, u32[]{:S(2)}, u32[]{:S(2)}) collective-permute-start(bf16[256,1024]{1,0:T(8,128)(2,1)S(1)} %copy-done.29), channel_id=1, source_target_pairs={{0,2},{1,3},{2,0},{3,1},{4,6},{5,7},{6,4},{7,5},{8,10},{9,11},{10,... | collective-permute-start | bytes 1572872 | tf_op jit(solution)/shard_map/ppermute | solution.py:30
  138.8 6.8 %collective-permute-start.35 = (bf16[2,64,256]{2,1,0:T(8,128)(2,1)S(1)}, bf16[2,64,256]{2,1,0:T(8,128)(2,1)S(1)}, u32[]{:S(2)}, u32[]{:S(2)}) collective-permute-start(bf16[2,64,256]{2,1,0:T(8,128)(2,1)S(1)} %bitcast.52), channel_id=1, source_target_pairs={{0,96},{4,100},{8,104},{12,108},{16,112},{20,116},{24,120},{28,124... | collective-permute-start | bytes 196616 | tf_op jit(solution)/shard_map/ppermute | solution.py:26
  140.8 7.6 %collective-permute-start.33 = (bf16[2,64,256]{2,1,0:T(8,128)(2,1)S(1)}, bf16[2,64,256]{2,1,0:T(8,128)(2,1)S(1)}, u32[]{:S(2)}, u32[]{:S(2)}) collective-permute-start(bf16[2,64,256]{2,1,0:T(8,128)(2,1)S(1)} %bitcast.51), channel_id=1, source_target_pairs={{0,64},{4,68},{8,72},{12,76},{16,80},{20,84},{24,88},{28,92},{32,9... | collective-permute-start | bytes 196616 | tf_op jit(solution)/shard_map/ppermute | solution.py:26
  141.9 6.4 %collective-permute-start.34 = (bf16[2,64,256]{2,1,0:T(8,128)(2,1)S(1)}, bf16[2,64,256]{2,1,0:T(8,128)(2,1)S(1)}, u32[]{:S(2)}, u32[]{:S(2)}) collective-permute-start(bf16[2,64,256]{2,1,0:T(8,128)(2,1)S(1)} %bitcast.50), channel_id=1, source_target_pairs={{0,32},{4,36},{8,40},{12,44},{16,48},{20,52},{24,56},{28,60},{32,0... | collective-permute-start | bytes 196616 | tf_op jit(solution)/shard_map/ppermute | solution.py:26
  152.9 7.9 %collective-permute-start.36 = (bf16[64,256]{1,0:T(8,128)(2,1)S(1)}, bf16[64,256]{1,0:T(8,128)(2,1)S(1)}, u32[]{:S(2)}, u32[]{:S(2)}) collective-permute-start(bf16[64,256]{1,0:T(8,128)(2,1)S(1)} %fusion.15), channel_id=1, source_target_pairs={{0,128},{4,132},{8,136},{12,140},{16,144},{20,148},{24,152},{28,15... | collective-permute-start | bytes 98312 | tf_op jit(solution)/shard_map/ppermute | solution.py:26
  161.7 9.0 %collective-permute-start.39 = (f32[64,256]{1,0:T(8,128)S(1)}, f32[64,256]{1,0:T(8,128)S(1)}, u32[]{:S(2)}, u32[]{:S(2)}) collective-permute-start(f32[64,256]{1,0:T(8,128)S(1)} %fusion.14), channel_id=1, source_target_pairs={{0,3},{1,2},{2,1},{3,0},{4,7},{5,6},{6,5},{7,4},{8,11},{9,10},{10,... | collective-permute-start | bytes 196616 | tf_op jit(solution)/shard_map/ppermute | solution.py:30
  163.0 7.7 %collective-permute-start.38 = (f32[64,256]{1,0:T(8,128)S(1)}, f32[64,256]{1,0:T(8,128)S(1)}, u32[]{:S(2)}, u32[]{:S(2)}) collective-permute-start(f32[64,256]{1,0:T(8,128)S(1)} %fusion.14), channel_id=1, source_target_pairs={{0,2},{1,3},{2,0},{3,1},{4,6},{5,7},{6,4},{7,5},{8,10},{9,11},{10,... | collective-permute-start | bytes 196616 | tf_op jit(solution)/shard_map/ppermute | solution.py:30
  163.0 7.7 %collective-permute-start.37 = (f32[64,256]{1,0:T(8,128)S(1)}, f32[64,256]{1,0:T(8,128)S(1)}, u32[]{:S(2)}, u32[]{:S(2)}) collective-permute-start(f32[64,256]{1,0:T(8,128)S(1)} %fusion.14), channel_id=1, source_target_pairs={{0,1},{1,0},{2,3},{3,2},{4,5},{5,4},{6,7},{7,6},{8,9},{9,8},{10,11... | collective-permute-start | bytes 196616 | tf_op jit(solution)/shard_map/ppermute | solution.py:30
  (26 other events, 87.7 us)
